TPU v7x, 32 devices: a whole 2x2x4 slice. The times are simulated.
32 devices in a mesh: batch: 8 (over y, x, core), tensor: 4 (over z).
Axes of the slice: x: 2, y: 2, z: 4, core: 2. Of those that a mesh axis runs over, the one named last changes fastest.
Arguments:
- hidden_in: bfloat16 [16384, 1024], P('batch'), may hold values from -6 to 6
- skip_state: bfloat16 [16384, 1024], P('batch'), may hold values from -6 to 6
- lengths: int32 [16], P('batch'), may hold values from 64 to 1024, as said below
- w_skip: bfloat16 [2048, 1024], P('tensor'), may hold values from -0.125 to 0.125
- b_skip: float32 [1024], replicated, may hold values from -3 to 3
- norm1_gain: float32 [1024], replicated, may hold values from 0.25 to 1.75
- norm1_bias: float32 [1024], replicated, may hold values from -3 to 3
- w_qkv: bfloat16 [3, 1024, 1024], P(None, None, 'tensor'), may hold values from -0.1875 to 0.1875
- b_qv: float32 [2, 1024], P(None, 'tensor'), may hold values from -3 to 3
- w_out: bfloat16 [1024, 1024], P('tensor'), may hold values from -0.5 to 0.5
- b_out: float32 [1024], replicated, may hold values from -3 to 3
- norm2_gain: float32 [1024], replicated, may hold values from 0.25 to 1.75
- norm2_bias: float32 [1024], replicated, may hold values from -3 to 3
- w_up: bfloat16 [1024, 4096], P(None, 'tensor'), may hold values from -0.1875 to 0.1875
- b_up: float32 [4096], P('tensor'), may hold values from -3 to 3
- w_down: bfloat16 [4096, 1024], P('tensor'), may hold values from -0.09375 to 0.09375
- b_down: float32 [1024], replicated, may hold values from -3 to 3
- cotangent: bfloat16 [16384, 1024], P('batch'), may hold values from -6 to 6
Outputs:
- output: bfloat16 [16384, 1024], P('batch')
- grad_hidden: bfloat16 [16384, 1024], P('batch')
- grad_skip: bfloat16 [16384, 1024], P('batch')
- grad_w_skip: float32 [2048, 1024], P('tensor')
- grad_b_skip: float32 [1024], replicated
- grad_norm1_gain: float32 [1024], replicated
- grad_norm1_bias: float32 [1024], replicated
- grad_w_qkv: float32 [3, 1024, 1024], P(None, None, 'tensor')
- grad_b_qv: float32 [2, 1024], P(None, 'tensor')
- grad_w_out: float32 [1024, 1024], P('tensor')
- grad_b_out: float32 [1024], replicated
- grad_norm2_gain: float32 [1024], replicated
- grad_norm2_bias: float32 [1024], replicated
- grad_w_up: float32 [1024, 4096], P(None, 'tensor')
- grad_b_up: float32 [4096], P('tensor')
- grad_w_down: float32 [4096, 1024], P('tensor')
- grad_b_down: float32 [1024], replicated
Inputs may be any that keep to these rules, and one draw needn't show every extreme that they name: `lengths`: frames of each utterance, each padded to 1024 slots; in every draw exactly one utterance of all 16 has 1024 frames and one has 64.
All inputs are finite; a program needn't handle non-finite values.
Results may differ from a plain program's by a relative error of at most 0.035.
Values may be sent and summed in bfloat16 or wider, within the bound.
No kernel may reach another device: no remote copies, remote signals or barrier semaphores. Data moves between devices by JAX's collectives and lax.ppermute only.
A program may use at most 256 MiB of HBM per device.

v0:
```python
import jax
import jax.numpy as jnp
from jax import lax
from jax.sharding import PartitionSpec as P

HEADS = 16
HEAD_DIM = 64


norm_eps = 1e-05
masked_score = -1e30


def layer_norm(values, gain, shift):
    centred = values - jnp.mean(values, axis=-1, keepdims=True)
    variance = jnp.mean(centred * centred, axis=-1, keepdims=True)
    return centred * lax.rsqrt(variance + norm_eps) * gain + shift


def gelu_tanh(values):
    return jax.nn.gelu(values, approximate=True)


def alibi_slopes(first_head, head_count):
    head_index = first_head + jnp.arange(head_count, dtype=jnp.int32) + 1
    return jnp.exp2(-8.0 * head_index.astype(jnp.float32) / HEADS)


def biased_scores(query_block, key_utt, first_row, first_head, key_valid):
    block_rows = query_block.shape[0]
    key_count = key_utt.shape[0]
    head_count = query_block.shape[1]
    products = jnp.einsum(
        "qhe,khe->hqk", query_block, key_utt, preferred_element_type=jnp.float32
    ) * HEAD_DIM ** (-0.5)
    query_pos = first_row + jnp.arange(block_rows, dtype=jnp.int32)
    key_pos = jnp.arange(key_count, dtype=jnp.int32)
    distance = jnp.abs(query_pos[:, None] - key_pos[None, :]).astype(jnp.float32)
    slopes = alibi_slopes(first_head, head_count)
    shifted = products - slopes[:, None, None] * distance[None]
    return jnp.where(key_valid[None, None, :], shifted, masked_score)


def body(
    hidden_in,
    skip_state,
    lengths,
    w_skip,
    b_skip,
    norm1_gain,
    norm1_bias,
    w_qkv,
    b_qv,
    w_out,
    b_out,
    norm2_gain,
    norm2_bias,
    w_up,
    b_up,
    w_down,
    b_down,
    cotangent,
):
    shard = lax.axis_index("tensor")
    row_count = hidden_in.shape[0]
    feature_width = hidden_in.shape[1]
    utt_count = lengths.shape[0]
    seq_len = row_count // utt_count
    block_rows = min(512, seq_len)
    block_count = seq_len // block_rows
    feature_block = w_skip.shape[0]
    column_block = w_out.shape[0]
    heads_local = column_block // HEAD_DIM
    first_head = shard * heads_local
    score_scale = HEAD_DIM ** (-0.5)
    joined = jnp.concatenate([hidden_in, skip_state], axis=1)
    features = lax.dynamic_slice_in_dim(joined, shard * feature_block, feature_block, 1)
    whole_skip = lax.all_gather(w_skip, "tensor", axis=0, tiled=True)
    skip_total = jnp.zeros((row_count, feature_width), jnp.float32)
    for feature_index in range(lax.axis_size("tensor")):
        first_feature = feature_index * feature_block
        partial_term = jnp.dot(
            joined[:, first_feature : first_feature + feature_block],
            whole_skip[first_feature : first_feature + feature_block],
            preferred_element_type=jnp.float32,
        )
        skip_total = skip_total + partial_term.astype(jnp.bfloat16).astype(jnp.float32)
    state_zero = skip_total + b_skip
    normed_one, norm1_back = jax.vjp(layer_norm, state_zero, norm1_gain, norm1_bias)
    normed_one = normed_one.astype(jnp.bfloat16)
    projected = jnp.einsum("td,sdc->stc", normed_one, w_qkv, preferred_element_type=jnp.float32)
    queries = (projected[0] + b_qv[0]).astype(jnp.bfloat16)
    keys_all = projected[1].astype(jnp.bfloat16)
    values_all = (projected[2] + b_qv[1]).astype(jnp.bfloat16)
    shape_heads = (utt_count, seq_len, heads_local, HEAD_DIM)
    query_view = queries.reshape(shape_heads)
    key_view = keys_all.reshape(shape_heads)
    value_view = values_all.reshape(shape_heads)

    def attend(item):
        query_utt, key_utt, value_utt, length_utt = item
        key_valid = jnp.arange(seq_len, dtype=jnp.int32) < length_utt
        mixed_blocks = []
        total_blocks = []
        for block_index in range(block_count):
            first_row = block_index * block_rows
            query_block = query_utt[first_row : first_row + block_rows]
            scores = biased_scores(query_block, key_utt, first_row, first_head, key_valid)
            highest_score = jnp.max(scores, axis=-1, keepdims=True)
            exponent = jnp.exp(scores - highest_score)
            totals = jnp.sum(exponent, axis=-1, keepdims=True)
            weights = (exponent / totals).astype(jnp.bfloat16)
            query_valid = first_row + jnp.arange(block_rows, dtype=jnp.int32) < length_utt
            mixed = jnp.einsum(
                "hqk,khe->qhe", weights, value_utt, preferred_element_type=jnp.float32
            )
            mixed_blocks.append(mixed * query_valid[:, None, None].astype(jnp.float32))
            total_blocks.append((highest_score + jnp.log(totals))[..., 0])
        return (jnp.concatenate(mixed_blocks, axis=0), jnp.concatenate(total_blocks, axis=1))

    mixed_all, log_totals = lax.map(attend, (query_view, key_view, value_view, lengths))
    mixed_all = mixed_all.reshape(row_count, column_block).astype(jnp.bfloat16)
    attn_term = jnp.dot(mixed_all, w_out, preferred_element_type=jnp.float32)
    state_one = (
        state_zero + lax.psum(attn_term.astype(jnp.bfloat16), "tensor").astype(jnp.float32) + b_out
    )
    normed_two, norm2_back = jax.vjp(layer_norm, state_one, norm2_gain, norm2_bias)
    normed_two = normed_two.astype(jnp.bfloat16)
    pre_act = jnp.dot(normed_two, w_up, preferred_element_type=jnp.float32) + b_up
    activated, gelu_back = jax.vjp(gelu_tanh, pre_act)
    activated = activated.astype(jnp.bfloat16)
    ffn_term = jnp.dot(activated, w_down, preferred_element_type=jnp.float32)
    output = (
        state_one + lax.psum(ffn_term.astype(jnp.bfloat16), "tensor").astype(jnp.float32) + b_down
    ).astype(jnp.bfloat16)
    upstream = cotangent.astype(jnp.float32)
    grad_b_down = jnp.sum(upstream, axis=0)
    grad_w_down = jnp.einsum("tf,td->fd", activated, cotangent, preferred_element_type=jnp.float32)
    grad_act = jnp.einsum("td,fd->tf", cotangent, w_down, preferred_element_type=jnp.float32)
    grad_pre = gelu_back(grad_act)[0].astype(jnp.bfloat16)
    grad_w_up = jnp.einsum("td,tf->df", normed_two, grad_pre, preferred_element_type=jnp.float32)
    grad_b_up = jnp.sum(grad_pre, axis=0, dtype=jnp.float32)
    normed_grad_two = jnp.einsum("tf,df->td", grad_pre, w_up, preferred_element_type=jnp.float32)
    grad_normed_two = lax.psum(normed_grad_two.astype(jnp.bfloat16), "tensor").astype(jnp.float32)
    grad_state_norm, grad_norm2_gain, grad_norm2_bias = norm2_back(grad_normed_two)
    grad_state_one = upstream + grad_state_norm
    grad_b_out = jnp.sum(grad_state_one, axis=0)
    state_half = grad_state_one.astype(jnp.bfloat16)
    grad_w_out = jnp.einsum("tc,td->cd", mixed_all, state_half, preferred_element_type=jnp.float32)
    grad_mixed = jnp.einsum(
        "td,cd->tc", state_half, w_out, preferred_element_type=jnp.float32
    ).astype(jnp.bfloat16)
    grad_mixed_view = grad_mixed.reshape(shape_heads)

    def attend_back(item):
        query_utt, key_utt, value_utt, grad_utt, total_utt, length_utt = item
        key_valid = jnp.arange(seq_len, dtype=jnp.int32) < length_utt
        grad_keys = jnp.zeros(key_utt.shape, jnp.float32)
        grad_values = jnp.zeros(value_utt.shape, jnp.float32)
        query_grads = []
        for block_index in range(block_count):
            first_row = block_index * block_rows
            query_block = query_utt[first_row : first_row + block_rows]
            query_valid = first_row + jnp.arange(block_rows, dtype=jnp.int32) < length_utt
            grad_block = grad_utt[first_row : first_row + block_rows] * query_valid[
                :, None, None
            ].astype(jnp.bfloat16)
            scores = biased_scores(query_block, key_utt, first_row, first_head, key_valid)
            weights = jnp.exp(scores - total_utt[:, first_row : first_row + block_rows][..., None])
            grad_weights = jnp.einsum(
                "qhe,khe->hqk", grad_block, value_utt, preferred_element_type=jnp.float32
            )
            inner = jnp.sum(weights * grad_weights, axis=-1, keepdims=True)
            grad_scores = (weights * (grad_weights - inner)).astype(jnp.bfloat16)
            query_grads.append(
                jnp.einsum("hqk,khe->qhe", grad_scores, key_utt, preferred_element_type=jnp.float32)
                * score_scale
            )
            grad_keys = (
                grad_keys
                + jnp.einsum(
                    "hqk,qhe->khe", grad_scores, query_block, preferred_element_type=jnp.float32
                )
                * score_scale
            )
            grad_values = grad_values + jnp.einsum(
                "hqk,qhe->khe",
                weights.astype(jnp.bfloat16),
                grad_block,
                preferred_element_type=jnp.float32,
            )
        return (jnp.concatenate(query_grads, axis=0), grad_keys, grad_values)

    grad_queries, grad_keys, grad_values = lax.map(
        attend_back, (query_view, key_view, value_view, grad_mixed_view, log_totals, lengths)
    )
    grad_proj = jnp.stack(
        [
            grad_queries.reshape(row_count, column_block),
            grad_keys.reshape(row_count, column_block),
            grad_values.reshape(row_count, column_block),
        ]
    ).astype(jnp.bfloat16)
    grad_w_qkv = jnp.einsum(
        "td,stc->sdc", normed_one, grad_proj, preferred_element_type=jnp.float32
    )
    grad_b_qv = jnp.stack(
        [
            jnp.sum(grad_proj[0], axis=0, dtype=jnp.float32),
            jnp.sum(grad_proj[2], axis=0, dtype=jnp.float32),
        ]
    )
    normed_grad_one = jnp.einsum(
        "stc,sdc->td", grad_proj, w_qkv, preferred_element_type=jnp.float32
    )
    grad_normed_one = lax.psum(normed_grad_one.astype(jnp.bfloat16), "tensor").astype(jnp.float32)
    grad_state_first, grad_norm1_gain, grad_norm1_bias = norm1_back(grad_normed_one)
    grad_state_zero = grad_state_one + grad_state_first
    grad_b_skip = jnp.sum(grad_state_zero, axis=0)
    zero_half = grad_state_zero.astype(jnp.bfloat16)
    grad_w_skip = jnp.einsum("tp,td->pd", features, zero_half, preferred_element_type=jnp.float32)
    grad_joined = jnp.einsum(
        "td,pd->tp", zero_half, whole_skip, preferred_element_type=jnp.float32
    ).astype(jnp.bfloat16)
    grad_hidden = grad_joined[:, :feature_width]
    grad_skip = grad_joined[:, feature_width:]
    (
        grad_w_skip,
        grad_b_skip,
        grad_norm1_gain,
        grad_norm1_bias,
        grad_w_qkv,
        grad_b_qv,
        grad_w_out,
        grad_b_out,
        grad_norm2_gain,
        grad_norm2_bias,
        grad_w_up,
        grad_b_up,
        grad_w_down,
        grad_b_down,
    ) = (
        lax.psum(grad_w_skip.astype(jnp.bfloat16), "batch").astype(jnp.float32),
        lax.psum(grad_b_skip.astype(jnp.bfloat16), "batch").astype(jnp.float32),
        lax.psum(grad_norm1_gain.astype(jnp.bfloat16), "batch").astype(jnp.float32),
        lax.psum(grad_norm1_bias.astype(jnp.bfloat16), "batch").astype(jnp.float32),
        lax.psum(grad_w_qkv.astype(jnp.bfloat16), "batch").astype(jnp.float32),
        lax.psum(grad_b_qv.astype(jnp.bfloat16), "batch").astype(jnp.float32),
        lax.psum(grad_w_out.astype(jnp.bfloat16), "batch").astype(jnp.float32),
        lax.psum(grad_b_out.astype(jnp.bfloat16), "batch").astype(jnp.float32),
        lax.psum(grad_norm2_gain.astype(jnp.bfloat16), "batch").astype(jnp.float32),
        lax.psum(grad_norm2_bias.astype(jnp.bfloat16), "batch").astype(jnp.float32),
        lax.psum(grad_w_up.astype(jnp.bfloat16), "batch").astype(jnp.float32),
        lax.psum(grad_b_up.astype(jnp.bfloat16), "batch").astype(jnp.float32),
        lax.psum(grad_w_down.astype(jnp.bfloat16), "batch").astype(jnp.float32),
        lax.psum(grad_b_down.astype(jnp.bfloat16), "batch").astype(jnp.float32),
    )
    return (
        output,
        grad_hidden,
        grad_skip,
        grad_w_skip,
        grad_b_skip,
        grad_norm1_gain,
        grad_norm1_bias,
        grad_w_qkv,
        grad_b_qv,
        grad_w_out,
        grad_b_out,
        grad_norm2_gain,
        grad_norm2_bias,
        grad_w_up,
        grad_b_up,
        grad_w_down,
        grad_b_down,
    )


def solution(mesh):
    placed = (
        P("batch", None),
        P("batch", None),
        P("batch"),
        P("tensor", None),
        P(),
        P(),
        P(),
        P(None, None, "tensor"),
        P(None, "tensor"),
        P("tensor", None),
        P(),
        P(),
        P(),
        P(None, "tensor"),
        P("tensor"),
        P("tensor", None),
        P(),
        P("batch", None),
    )
    return jax.shard_map(
        body,
        mesh=mesh,
        in_specs=placed,
        out_specs=(
            P("batch", None),
            P("batch", None),
            P("batch", None),
            P("tensor", None),
            P(),
            P(),
            P(),
            P(None, None, "tensor"),
            P(None, "tensor"),
            P("tensor", None),
            P(),
            P(),
            P(),
            P(None, "tensor"),
            P("tensor"),
            P("tensor", None),
            P(),
        ),
        check_vma=False,
    )
```

profile of v0, /device:TPU:0, one launch (start us, length us, event | category | flops | bytes accessed | tf_op | source)
XLA Modules:
  0.0 1105.6 jit_solution(11440639583085087926)
XLA Ops:
  8.9 84.2 %all-gather.2.cloned.1.call-done = bf16[2048,1024]{1,0:T(8,128)(2,1)} async-done(((bf16[512,1024]{1,0:T(8,128)(2,1)}), bf16[2048,1024]{1,0:T(8,128)(2,1)}) %all-gather.2.cloned.1.call-update) | async-done | bytes 4194320 | tf_op jit(solution)/shard_map/all_gather | solution.py:78
  93.1 6.4 fusion.113
  99.5 4.4 fusion.115
  103.9 4.4 fusion.111
  108.3 6.4 fusion.142
  117.4 4.3 convolution_bitcast_fusion
  124.1 2.9 copy.55
  127.0 4.0 squeeze.60
  136.5 2.9 copy.59
  139.4 2.9 copy.54
  142.3 4.4 squeeze.59
  151.4 43.2 %while.30 = (s32[]{:T(128)}, bf16[2,1024,4,64]{1,3,2,0:T(8,128)(2,1)}, f32[2,4,1024]{2,1,0:T(4,128)S(1)}, bf16[2,1024,4,64]{1,3,2,0:T(8,128)(2,1)}, s32[2]{0:T(1...) while((s32[]{:T(128)}, ...), condition=%wide.region_7.8_spmd, body=%wide.region_2.7_spmd.sunk | while | flops 1153961984 | bytes 84073232 | solution.py:121
  154.1 3.3 fusion.206
  157.4 5.7 fusion.207
  163.0 3.1 fusion.211
  168.8 3.0 fusion.210
  175.6 3.3 fusion.206
  178.9 5.7 fusion.207
  184.6 3.1 fusion.211
  190.3 3.0 fusion.210
  198.2 4.4 convolution_convert_fusion.1
  202.6 153.6 %all-reduce.8.cloned.1.call-done = bf16[2048,1024]{0,1:T(8,128)(2,1)} async-done(((bf16[2048,1024]{0,1:T(8,128)(2,1)}), bf16[2048,1024]{0,1:T(8,128)(2,1)}) %all-reduce.8.cloned.1.call-update) | async-done | bytes 4194320 | tf_op jit(solution)/shard_map/psum | solution.py:125
  356.2 5.7 fusion.138
  367.5 4.7 fusion.143
  372.2 10.5 fusion.136
  384.8 6.2 convolution_convert_fusion.2
  391.0 7.0 copy.63
  398.0 10.3 convolution_convert_fusion.3
  408.3 136.9 %all-reduce.10.cloned.1.call-done = bf16[2048,1024]{0,1:T(8,128)(2,1)} async-done(((bf16[2048,1024]{0,1:T(8,128)(2,1)}), bf16[2048,1024]{0,1:T(8,128)(2,1)}) %all-reduce.10.cloned.1.call-update) | async-done | bytes 4194320 | tf_op jit(solution)/shard_map/psum | solution.py:144
  545.1 5.7 fusion.91
  550.9 7.6 fusion.92
  558.6 3.6 add_add_fusion.3
  562.2 3.2 copy-done.4
  567.8 3.3 reshape.304
  576.7 49.1 %while.31 = (s32[]{:T(128)}, bf16[2,1024,4,64]{1,3,2,0:T(8,128)(2,1)}, bf16[2,1024,4,64]{1,3,2,0:T(8,128)(2,1)}, bf16[2,1024,4,64]{1,3,2,0:T(8,128)(2,1)}, bf16[...) while((s32[]{:T(128)}, ...), condition=%wide.region_18.19_spmd, body=%wide.region_15.18_spmd.sunk | while | flops 2737307648 | bytes 186259456 | solution.py:194
  582.0 3.4 multiply_reduce_fusion.6
  590.9 3.3 multiply_reduce_fusion.7
  606.3 3.4 multiply_reduce_fusion.6
  615.2 3.3 multiply_reduce_fusion.7
  625.9 2.9 copy.91
  630.9 2.9 copy.93
  635.2 2.9 copy.92
  644.6 6.4 bitcast_convert_fusion
  651.1 2.9 reduce_sum.271
  654.0 10.2 convolution_convert_fusion.6
  664.2 11.1 %convolution_convert_fusion.5 = bf16[1024,1024]{1,0:T(8,128)(2,1)} fusion(bf16[2048,1024]{1,0:T(8,128)(2,1)S(1)} %copy-done.13, f32[2048,1024]{1,0:T(8,128)} %copy-done.58, f32[1024]{0:T(1024)S(1)} %copy-done.53), kind=kOutput, calls=%fused_computation.177 | convolution fusion | flops 4316987392 | bytes 14684160 | tf_op jit(solution)/shard_map/tf,td->fd/dot_general | solution.py:138
  676.0 2.9 reduce_sum.269
  678.9 5.7 fusion.122
  684.6 8.8 fusion.117
  693.4 248.3 %all-reduce.14.cloned.1.call-done = (bf16[2048,1024]{0,1:T(8,128)(2,1)}, bf16[2048,1024]{0,1:T(8,128)(2,1)}) async-done(((bf16[2048,1024]{0,1:T(8,128)(2,1)}, bf16[2048,1024]{0,1:T(8,128)(2,1)}), (bf16[2048,1024]{0,1:T(8,128)(2,1)}, bf16[2048,1024]{0,1:T(8,128)(2,1)})) %all-reduce.14.cloned.1.call-update) | async-done | bytes 8388624 | tf_op jit(solution)/shard_map/psum | solution.py:216
  941.7 5.7 fusion.90
  947.5 5.7 fusion.135
  955.1 6.6 fusion.93
  961.7 6.2 fusion.118
  967.9 7.6 add_convert_fusion
  975.5 6.4 copy.79
  981.9 2.8 reduce_sum.264
  984.7 25.9 %all-reduce = (bf16[1024]{0:T(1024)(128)(2,1)S(1)}, bf16[1024]{0:T(1024)(128)(2,1)S(1)}, bf16[1024]{0:T(1024)(128)(2,1)S(1)}, bf16[2,256]{1,0:T(2,128)(2,1)S(1)}...) all-reduce(bf16[1024]{0:T(1024)(128)(2,1)S(1)} %get-tuple-element.3, ...), channel_id=1, replica_groups=mesh['batch'=8,'tensor'=4] {'batch'}, use_global_device_ids=true, to_apply=%region_24.25 | all-reduce | flops 8704 | bytes 34816 | tf_op jit(solution)/shard_map/psum | solution.py:244
  1016.0 12.1 %convolution_convert_fusion = bf16[2048,2048]{1,0:T(8,128)(2,1)S(1)} fusion(bf16[2048,1024]{0,1:T(8,128)(2,1)} %get-tuple-element.419, bf16[2048,1024]{1,0:T(8,128)(2,1)} %all-gather.2.cloned.1.call-done), kind=kOutput, calls=%fused_computation.153 | convolution fusion | flops 8594128896 | bytes 16777216 | tf_op jit(solution)/shard_map/td,pd->tp/dot_general | solution.py:222
  1028.1 3.9 fusion.140
  1032.0 52.0 %all-reduce.12.cloned.1.call-done = (bf16[3,1024,256]{1,2,0:T(8,128)(2,1)}, bf16[512,1024]{1,0:T(8,128)(2,1)}, bf16[256,1024]{1,0:T(8,128)(2,1)}, bf16[1024,1024]{1,0:T(8,128)(2,1)}, bf16[1024,1024]{1,0:T(8,128)(2,1)}) async-done(((bf16[3,1024,256]{1,2,0:T(8,128)(2,1)}, bf16[512,1024]{1,0:T(8,128)(2,1)}, bf16[256,1024]{1,0:T(8,128)(2,1)}, bf16[1024,1024]{1,0:T(8,128)(2,1)}, bf16[1024,1024]{1,0:T(8,128)(2,1)}), ...) | async-done | bytes 7340048 | tf_op jit(solution)/shard_map/psum | solution.py:247
  1086.2 3.2 copy.80
  1089.4 2.9 convert_element_type.358
  1092.3 4.1 convert_element_type.378
  (284 shorter events, 106.4 us)
Async XLA Ops:
  7.2 365.0 %copy-start = (bf16[1024,1024]{1,0:T(8,128)(2,1)S(1)}, bf16[1024,1024]{1,0:T(8,128)(2,1)}, u32[]{:S(2)}) copy-start(bf16[1024,1024]{1,0:T(8,128)(2,1)} %param.37) | copy-start | bytes 6291460
  7.2 85.9 %all-gather.2.cloned.1.call-start = ((), (), s32[]{:S(2)}) async-start(), calls=%async_computation | async-start | bytes 5242880 | tf_op jit(solution)/shard_map/all_gather | solution.py:78
  7.9 348.3 %all-reduce.8.cloned.1.call-start = ((), (), s32[]{:S(2)}) async-start(), calls=%async_computation.1 | async-start | bytes 8388608 | tf_op jit(solution)/shard_map/psum | solution.py:125
  93.1 6.4 copy-start.47
  93.1 6.4 copy-start.48
  99.5 4.4 copy-start.46
  103.9 4.4 copy-start.51
  103.9 4.4 copy-start.57
  114.8 7.0 copy-start.3
  114.8 2.1 copy-start.39
  114.8 2.6 copy-start.50
  114.8 2.6 copy-start.54
  136.5 15.0 %copy-start.56 = (s32[2]{0:T(128)S(1)}, s32[2]{0:T(128)}, u32[]{:S(2)}) copy-start(s32[2]{0:T(128)} %param.24) | copy-start | bytes 28
  157.3 5.7 copy-start.8
  168.8 3.1 copy-start.26
  178.9 5.7 copy-start.8
  190.3 3.1 copy-start.26
  194.6 161.6 %copy-start.44 = (f32[1024]{0:T(1024)S(1)}, f32[1024]{0:T(1024)}, u32[]{:S(2)}) copy-start(f32[1024]{0:T(1024)} %param.32) | copy-start | bytes 12292
  202.6 342.5 %all-reduce.10.cloned.1.call-start = ((), (), s32[]{:S(2)}) async-start(), calls=%async_computation.2 | async-start | bytes 8388608 | tf_op jit(solution)/shard_map/psum | solution.py:144
  361.9 3.6 copy-start.2
  362.8 4.7 copy-start.49
  365.5 2.0 copy-start.25
  367.5 4.7 copy-start.12
  367.5 4.7 copy-start.52
  372.2 10.5 copy-start.58
  382.8 2.0 copy-start.59
  391.0 550.7 %all-reduce.14.cloned.1.call-start = ((), (), s32[]{:S(2)}) async-start(), calls=%async_computation.4 | async-start | bytes 16777216 | tf_op jit(solution)/shard_map/psum | solution.py:216
  545.1 5.8 copy-start.5
  545.1 13.4 %slice-start = ((s8[8388608]{0:T(1024)(128)(4,1)}), s8[4194304]{0:T(1024)(128)(4,1)S(1)}, s32[]{:S(2)}) async-start(s8[8388608]{0:T(1024)(128)(4,1)} %bitcast.219), calls=%async_computation.5 | async-start | bytes 8388608
  550.8 7.7 copy-start.14
  550.9 7.6 slice-start.1
  558.5 6.9 copy-start.29
  562.2 3.2 copy-start.4
  576.9 5.1 copy-start.7
  586.7 3.0 copy-start.9
  590.9 3.3 copy-start.17
  596.1 2.3 copy-start.23
  597.5 1.8 copy-start.20
  601.2 5.1 copy-start.7
  610.9 3.0 copy-start.9
  615.2 3.3 copy-start.17
  620.4 2.3 copy-start.23
  651.0 433.0 %all-reduce.12.cloned.1.call-start = ((), (), s32[]{:S(2)}) async-start(), calls=%async_computation.3 | async-start | bytes 14680064 | tf_op jit(solution)/shard_map/psum | solution.py:247
  654.0 10.2 copy-start.13
  654.0 10.2 copy-start.53
  664.2 11.2 %copy-start.19 = (bf16[2,1024,4,64]{1,3,2,0:T(8,128)(2,1)S(1)}, bf16[2,1024,4,64]{1,3,2,0:T(8,128)(2,1)}, u32[]{:S(2)}) copy-start(bf16[2,1024,4,64]{1,3,2,0:T(8,128)(2,1)} %get-tuple-element.264) | copy-start | bytes 3145732
  664.2 11.5 %copy-start.22 = (bf16[2,1024,4,64]{1,3,2,0:T(8,128)(2,1)S(1)}, bf16[2,1024,4,64]{1,3,2,0:T(8,128)(2,1)}, u32[]{:S(2)}) copy-start(bf16[2,1024,4,64]{1,3,2,0:T(8,128)(2,1)} %get-tuple-element.262) | copy-start | bytes 3145732
  664.2 14.7 %copy-start.16 = (bf16[32,8,2,1024]{3,1,2,0:T(8,128)(2,1)S(1)}, bf16[32,8,2,1024]{3,1,2,0:T(8,128)(2,1)}, u32[]{:S(2)}) copy-start(bf16[32,8,2,1024]{3,1,2,0:T(8,128)(2,1)} %copy-done.15) | copy-start | bytes 3145732
  675.3 9.3 copy-start.33
  675.3 9.3 copy-start.35
  675.3 9.3 copy-start.40
  675.3 9.3 copy-start.55
  678.9 5.7 copy-start.31
  693.4 254.0 %copy-start.37 = (f32[2048]{0:T(1024)S(1)}, f32[2048]{0:T(1024)}, u32[]{:S(2)}) copy-start(f32[2048]{0:T(1024)} %copy-done.36) | copy-start | bytes 24580
  941.7 5.8 copy-start.6
  941.7 11.6 %slice-start.2 = ((s8[8388608]{0:T(1024)(128)(4,1)}), s8[4194304]{0:T(1024)(128)(4,1)S(1)}, s32[]{:S(2)}) async-start(s8[8388608]{0:T(1024)(128)(4,1)} %bitcast.221), calls=%async_computation.7 | async-start | bytes 8388608
  941.7 11.6 %slice-start.4 = ((s8[8388608]{0:T(1024)(128)(4,1)}), s8[4194304]{0:T(1024)(128)(4,1)S(1)}, s32[]{:S(2)}) async-start(s8[8388608]{0:T(1024)(128)(4,1)} %bitcast.223), calls=%async_computation.9 | async-start | bytes 8388608
  947.5 6.3 slice-start.3
  947.5 7.5 slice-start.5
  961.7 6.2 copy-start.43
  975.5 9.2 copy-start.41
  975.5 9.2 copy-start.45
  1086.1 12.7 %copy-start.1 = (bf16[1024,1024]{1,0:T(8,128)(2,1)S(1)}, bf16[1024,1024]{1,0:T(8,128)(2,1)}, u32[]{:S(2)}) copy-start(bf16[1024,1024]{1,0:T(8,128)(2,1)} %param.37) | copy-start | bytes 6291460
  1089.4 7.0 copy-start.28
  (20 other events, 22.6 us)
Sparse Core Ops, SparseCore 0:
  9.6 83.4 all-gather.1
  202.7 153.5 all-reduce.7
  391.1 153.9 all-reduce.9
  651.1 290.5 all-reduce.13
  968.0 115.9 all-reduce.11
where the time goes:
time: 1110 us
  waiting for transfers between devices  676 us (61%)
  matrix products  189 us (17%)
  other arithmetic  99.8 us (9%)
  local copies, waits for them, and re-layouts  98.5 us (9%)
  blocking collectives  25.9 us (2%)
  between operations  14.7 us (1%)
    psum x1, waiting for transfers between devices, body(): lax.psum(normed_grad_one.astype(jnp.bfloat16), 'tensor').astype(jnp.float32)  248 us
    psum x1, waiting for transfers between devices, body(): lax.psum(attn_term.astype(jnp.bfloat16), 'tensor').astype(jnp.float32)  154 us
    psum x1, waiting for transfers between devices, body(): lax.psum(normed_grad_two.astype(jnp.bfloat16), 'tensor').astype(jnp.float32)  137 us
    all_gather x1, waiting for transfers between devices, body(): whole_skip = lax.all_gather(w_skip, 'tensor', axis=0, tiled=True)  84.2 us
    psum x1, waiting for transfers between devices, body(): lax.psum(grad_w_qkv.astype(jnp.bfloat16), 'batch').astype(jnp.float32)  52 us
    unnamed x112, local copies, waits for them, and re-layouts  34.1 us
    reduce_sum x6, other arithmetic, layer_norm(): return centred * lax.rsqrt(variance + norm_eps) * gain + shift  31.3 us
    dot_general x8, matrix products, biased_scores(): jnp.einsum('qhe,khe->hqk', query_block, key_utt, preferred_element_type=j...  31.2 us
  transfers between devices with their start and end apart: 5, of which 5 were waited for; matrix products, arithmetic and copies ran while one was open for 9% of the time, Pallas kernels for 0%

commit v1 on v0

v1 whole, which is shorter than its diff:
```python
import functools

import jax
import jax.numpy as jnp
from jax import lax
from jax.experimental import pallas as pl
from jax.experimental.pallas import tpu as pltpu
from jax.sharding import PartitionSpec as P

HEADS = 16
HEAD_DIM = 64
GROUP = 8
TILE = 256
LOG2E = 1.4426950408889634
LN2 = 0.6931471805599453
GELU_C = 0.7978845608028654
GELU_A = 0.044715

norm_eps = 1e-05
masked_score = -1e30
bf16 = jnp.bfloat16
f32 = jnp.float32

NT = (((1,), (1,)), ((), ()))
TN = (((0,), (0,)), ((), ()))

PIECES = [0, 2, 4, 6, 1, 3, 5, 7]
COUNT = len(PIECES)


def dot(a, b):
    return jnp.dot(a, b, preferred_element_type=f32)


def dot_nt(a, b):
    return lax.dot_general(a, b, NT, preferred_element_type=f32)


def dot_tn(a, b):
    return lax.dot_general(a, b, TN, preferred_element_type=f32)


def params(ndim, mib=60):
    return pltpu.CompilerParams(
        vmem_limit_bytes=mib * 1024 * 1024, dimension_semantics=("arbitrary",) * ndim
    )


def cost(flops, moved):
    return pl.CostEstimate(flops=int(flops), bytes_accessed=int(moved), transcendentals=0)


def along(x, k):
    n = lax.axis_size("tensor")
    return lax.ppermute(x, "tensor", [(i, (i + k) % n) for i in range(n)])


def across(x, m):
    n = lax.axis_size("batch")
    return lax.ppermute(x, "batch", [(i, i ^ m) for i in range(n)])


def from_chips(held):
    return [held, across(held, 2), across(held, 4), across(held, 6)]


def from_cores(held):
    return held + [across(x, 1) for x in held]


def after(x, *earlier):
    return lax.optimization_barrier((x,) + earlier)[0]


def start_loads(info, refs, own, targets, sem):
    for first, rows, own_first, dest, place in targets:
        off = pl.multiple_of(place(info[0], 0), 16)
        pltpu.make_async_copy(
            own.at[pl.ds(own_first, rows * GROUP)], dest.at[pl.ds(off, rows * GROUP)], sem
        ).start()
    for ref, m in zip(refs, PIECES):
        for kk in range(3):
            src_t = (info[0] + 3 - kk) & 3
            src_b = info[1] ^ m
            for first, rows, _, dest, place in targets:
                off = pl.multiple_of(place(src_t, src_b), 16)
                pltpu.make_async_copy(
                    ref.at[kk, pl.ds(first, rows)], dest.at[pl.ds(off, rows)], sem
                ).start()


def wait_whole(dest, sem):
    pltpu.make_async_copy(dest, dest, sem).wait()


ANY = pl.BlockSpec(memory_space=pltpu.HBM)


def whole(shape):
    return pl.BlockSpec(shape, lambda *_: (0,) * len(shape))


def once(shape):
    return pl.BlockSpec(shape, lambda *_: (0,) * len(shape), pipeline_mode=pl.Buffered(1))


def normalise(v):
    mean = jnp.mean(v, axis=-1, keepdims=True)
    centred = v - mean
    r = lax.rsqrt(jnp.mean(centred * centred, axis=-1, keepdims=True) + norm_eps)
    return centred * r, r


def norm_back(grad, n, r, gain):
    e = grad * gain
    return r * (
        e
        - jnp.mean(e, axis=-1, keepdims=True)
        - n * jnp.mean(e * n, axis=-1, keepdims=True)
    )


def tile_length(info, i, tiles_per):
    u = i // tiles_per
    return (i - u * tiles_per) * TILE, info[2 + u]


def skip_targets(w):
    shard = w.shape[0] // 4
    piece = shard // GROUP
    return [(0, piece, 0, w, lambda t, b: t * shard + b * piece)]


def out_targets(w, first):
    shard = w.shape[0] // 4
    piece = shard // GROUP
    return [(first, piece, 0, w, lambda t, b: t * shard + b * piece)]


def skip_kernel(info, hid, skp, b_skip, gain, bias, *rest):
    own, refs, (state, normed, w, sem) = rest[0], rest[1 : 1 + COUNT], rest[1 + COUNT :]

    @pl.when(pl.program_id(0) == 0)
    def _():
        start_loads(info, refs, own, skip_targets(w), sem)
        wait_whole(w, sem)

    width = hid.shape[1]
    total = dot(hid[...], w[:width]) + dot(skp[...], w[width:]) + b_skip[...]
    state[...] = total.astype(bf16)
    n, _ = normalise(total)
    normed[...] = (n * gain[...] + bias[...]).astype(bf16)


def skip_call(info, hid, skp, b_skip, gain, bias, own, pieces):
    rows, d = hid.shape
    row = pl.BlockSpec((TILE, d), lambda i, s: (i, 0))
    return pl.pallas_call(
        skip_kernel,
        grid_spec=pltpu.PrefetchScalarGridSpec(
            num_scalar_prefetch=1,
            grid=(rows // TILE,),
            in_specs=[row, row, whole((1, d)), whole((1, d)), whole((1, d))] + [ANY] * (1 + COUNT),
            out_specs=[row, row],
            scratch_shapes=[pltpu.VMEM((2 * d, d), bf16), pltpu.SemaphoreType.DMA],
        ),
        out_shape=[jax.ShapeDtypeStruct((rows, d), bf16)] * 2,
        compiler_params=params(1),
        cost_estimate=cost(4 * rows * d * d, rows * d * 10 + 4 * d * d),
        name="skip_norm",
    )(info, hid, skp, b_skip, gain, bias, own, *pieces)


def qkv_targets(w):
    d = w.shape[0] // 3
    shard = d // 4
    part = shard // GROUP
    return [
        (s * part, part, s * shard, w, lambda t, b, s=s: s * d + t * shard + b * part)
        for s in range(3)
    ]


def qkv_kernel(tiles_per, info, x, b_q, b_v, *rest):
    own, refs, (q, k, v, w, sem) = rest[0], rest[1 : 1 + COUNT], rest[1 + COUNT :]
    i = pl.program_id(0)
    d = x.shape[1]

    @pl.when(i == 0)
    def _():
        start_loads(info, refs, own, qkv_targets(w), sem)
        wait_whole(w, sem)

    first, length = tile_length(info, i, tiles_per)

    @pl.when(first < length)
    def _():
        xs = x[...]
        q[...] = ((dot_nt(xs, w[:d]) + b_q[...]) * (LOG2E * HEAD_DIM**-0.5)).astype(bf16)
        k[...] = dot_nt(xs, w[d : 2 * d]).astype(bf16)
        v[...] = (dot_nt(xs, w[2 * d :]) + b_v[...]).astype(bf16)


def qkv_call(info, x, b_q, b_v, own, pieces, tiles_per):
    rows, d = x.shape
    row = pl.BlockSpec((TILE, d), lambda i, s: (i, 0))
    return pl.pallas_call(
        functools.partial(qkv_kernel, tiles_per),
        grid_spec=pltpu.PrefetchScalarGridSpec(
            num_scalar_prefetch=1,
            grid=(rows // TILE,),
            in_specs=[row, whole((1, d)), whole((1, d))] + [ANY] * (1 + COUNT),
            out_specs=[row] * 3,
            scratch_shapes=[pltpu.VMEM((3 * d, d), bf16), pltpu.SemaphoreType.DMA],
        ),
        out_shape=[jax.ShapeDtypeStruct((rows, d), bf16)] * 3,
        compiler_params=params(1),
        cost_estimate=cost(4 * rows * d * d, rows * d * 8 + 6 * d * d),
        name="qkv",
    )(info, x, b_q, b_v, own, *pieces)


def slope2(head):
    return jnp.exp2(jnp.full((1, 1), -8.0 / HEADS, f32) * (head + 1).astype(f32)) * LOG2E


def attend_kernel(info, q, k, v, mixed, lse, dist):
    u, hp = pl.program_id(0), pl.program_id(1)
    seq = q.shape[0]
    tiles = seq // TILE
    length = info[2 + u]

    @pl.when((u == 0) & (hp == 0))
    def _():
        r = lax.broadcasted_iota(jnp.int32, dist.shape, 0)
        c = lax.broadcasted_iota(jnp.int32, dist.shape, 1)
        dist[...] = jnp.abs(r - c + (seq - TILE)).astype(f32)

    lane = lax.broadcasted_iota(jnp.int32, (TILE, 128), 1)
    used = (length + TILE - 1) // TILE

    for n in range(1, tiles + 1):

        @pl.when(used == n)
        def _(n=n):
            cols = n * TILE
            valid = (
                lax.broadcasted_iota(jnp.int32, (TILE, TILE), 1) + (cols - TILE) < length
            )

            def step(i, carry):
                row0 = pl.multiple_of(i * TILE, TILE)
                qs = q[pl.ds(row0, TILE), :]
                start = pl.multiple_of((seq - TILE) - row0, TILE)
                gap = dist[:, pl.ds(start, cols)]
                outs, sums = [], []
                for a in range(2):
                    qa = jnp.where((lane < 64) == (a == 0), qs, jnp.zeros_like(qs))
                    s = dot_nt(qa, k[:cols, :]) - slope2(2 * hp + a) * gap
                    last = jnp.where(valid, s[:, cols - TILE :], masked_score)
                    s = jnp.concatenate([s[:, : cols - TILE], last], axis=1) if n > 1 else last
                    m = jnp.max(s, axis=1, keepdims=True)
                    p = jnp.exp2(s - m)
                    total = jnp.sum(p, axis=1, keepdims=True)
                    outs.append(dot(p.astype(bf16), v[:cols, :]) * (1.0 / total))
                    sums.append(m + jnp.log2(total))
                o = jnp.where(lane < 64, outs[0], outs[1])
                pos = lax.broadcasted_iota(jnp.int32, (TILE, 128), 0) + row0
                mixed[pl.ds(row0, TILE), :] = jnp.where(pos < length, o, 0.0).astype(bf16)
                old = lse[pl.ds(row0, TILE), :]
                new = jnp.where(lane == 2 * hp, sums[0], old)
                lse[pl.ds(row0, TILE), :] = jnp.where(lane == 2 * hp + 1, sums[1], new)
                return carry

            lax.fori_loop(0, n, step, 0)
            if n < tiles:
                mixed[cols:, :] = jnp.zeros((seq - cols, 128), bf16)


def attend_call(info, q, k, v, seq):
    rows, d = q.shape
    utts = rows // seq
    blk = pl.BlockSpec((seq, 128), lambda u, h, s: (u, h))
    return pl.pallas_call(
        attend_kernel,
        grid_spec=pltpu.PrefetchScalarGridSpec(
            num_scalar_prefetch=1,
            grid=(utts, d // 128),
            in_specs=[blk] * 3,
            out_specs=[blk, pl.BlockSpec((seq, 128), lambda u, h, s: (u, 0))],
            scratch_shapes=[pltpu.VMEM((TILE, 2 * seq - TILE), f32)],
        ),
        out_shape=[
            jax.ShapeDtypeStruct((rows, d), bf16),
            jax.ShapeDtypeStruct((rows, 128), f32),
        ],
        compiler_params=params(2),
        cost_estimate=cost(rows * seq * d * 4, rows * d * 8),
        name="attend",
    )(info, q, k, v)


def attend_back_kernel(info, q, k, v, g, o, lse, dq, dk, dv, dist, akey, aval):
    u, hp = pl.program_id(0), pl.program_id(1)
    seq = q.shape[0]
    tiles = seq // TILE
    length = info[2 + u]

    @pl.when((u == 0) & (hp == 0))
    def _():
        r = lax.broadcasted_iota(jnp.int32, dist.shape, 0)
        c = lax.broadcasted_iota(jnp.int32, dist.shape, 1)
        dist[...] = jnp.abs(r - c - (seq - TILE)).astype(f32)

    lane = lax.broadcasted_iota(jnp.int32, (TILE, 128), 1)
    used = (length + TILE - 1) // TILE

    for n in range(1, tiles + 1):

        @pl.when(used == n)
        def _(n=n):
            cols = n * TILE
            valid = (
                lax.broadcasted_iota(jnp.int32, (TILE, TILE), 0) + (cols - TILE) < length
            )
            akey[:cols, :] = jnp.zeros((cols, 128), f32)
            aval[:cols, :] = jnp.zeros((cols, 128), f32)
            klane = lax.broadcasted_iota(jnp.int32, (cols, 128), 1)

            def step(i, carry):
                row0 = pl.multiple_of(i * TILE, TILE)
                qs = q[pl.ds(row0, TILE), :]
                gs = g[pl.ds(row0, TILE), :]
                start = pl.multiple_of((seq - TILE) - row0, TILE)
                gap = dist[pl.ds(start, cols), :]
                both = gs.astype(f32) * o[pl.ds(row0, TILE), :].astype(f32)
                hi = both.astype(bf16)
                lo = (both - hi.astype(f32)).astype(bf16)
                grads = []
                for a in range(2):
                    mine = (lane < 64) == (a == 0)
                    qa = jnp.where(mine, qs, jnp.zeros_like(qs))
                    ga = jnp.where(mine, gs, jnp.zeros_like(gs))
                    pick = jnp.where(
                        (lax.broadcasted_iota(jnp.int32, (8, 128), 1) < 64) == (a == 0), 1.0, 0.0
                    ).astype(bf16)
                    delta = (dot_nt(pick, hi) + dot_nt(pick, lo))[:1, :]
                    row = lse[pl.ds(2 * hp + a, 1), pl.ds(row0, TILE)]
                    s = dot_nt(k[:cols, :], qa) - (slope2(2 * hp + a) * gap + row)
                    last = jnp.where(valid, s[cols - TILE :, :], masked_score)
                    s = jnp.concatenate([s[: cols - TILE, :], last], axis=0) if n > 1 else last
                    p = jnp.exp2(s)
                    gw = dot_nt(v[:cols, :], ga)
                    ds = (p * (gw - delta)).astype(bf16)
                    aval[:cols, :] += dot(p.astype(bf16), ga)
                    akey[:cols, :] += dot(ds, qa)
                    ka = k[:cols, :]
                    ka = jnp.where((klane < 64) == (a == 0), ka, jnp.zeros_like(ka))
                    grads.append(dot_tn(ds, ka))
                dq[pl.ds(row0, TILE), :] = ((grads[0] + grads[1]) * HEAD_DIM**-0.5).astype(bf16)
                return carry

            lax.fori_loop(0, n, step, 0)
            dk[:cols, :] = (akey[:cols, :] * LN2).astype(bf16)
            dv[:cols, :] = aval[:cols, :].astype(bf16)
            if n < tiles:
                for ref in (dq, dk, dv):
                    ref[cols:, :] = jnp.zeros((seq - cols, 128), bf16)


def attend_back_call(info, q, k, v, g, o, lse, seq):
    rows, d = q.shape
    utts = rows // seq
    blk = pl.BlockSpec((seq, 128), lambda u, h, s: (u, h))
    return pl.pallas_call(
        attend_back_kernel,
        grid_spec=pltpu.PrefetchScalarGridSpec(
            num_scalar_prefetch=1,
            grid=(utts, d // 128),
            in_specs=[blk] * 5 + [pl.BlockSpec((HEADS, seq), lambda u, h, s: (0, u))],
            out_specs=[blk] * 3,
            scratch_shapes=[
                pltpu.VMEM((2 * seq - TILE, TILE), f32),
                pltpu.VMEM((seq, 128), f32),
                pltpu.VMEM((seq, 128), f32),
            ],
        ),
        out_shape=[jax.ShapeDtypeStruct((rows, d), bf16)] * 3,
        compiler_params=params(2),
        cost_estimate=cost(rows * seq * d * 10, rows * d * 16),
        name="attend_back",
    )(info, q, k, v, g, o, lse)


def mix_kernel(tiles_per, info, mixed, state, b_out, gain, bias, *rest):
    own, refs, (state_one, normed, w, total, sem) = rest[0], rest[1 : 1 + COUNT], rest[1 + COUNT :]
    part = (own.shape[0] // GROUP) * 2
    i = pl.program_id(0)
    d = mixed.shape[1]

    @pl.when(i == 0)
    def _():
        start_loads(info, refs, own, out_targets(w, part), sem)
        wait_whole(w, sem)

    first, length = tile_length(info, i, tiles_per)
    total[...] = state[...].astype(f32) + b_out[...]

    @pl.when(first < length)
    def _():
        total[...] += dot(mixed[...], w[...])

    n, _ = normalise(total[...])
    state_one[...] = total[...].astype(bf16)
    normed[...] = (n * gain[...] + bias[...]).astype(bf16)


def mix_call(info, mixed, state, b_out, gain, bias, own, pieces, tiles_per):
    rows, d = mixed.shape
    row = pl.BlockSpec((TILE, d), lambda i, s: (i, 0))
    return pl.pallas_call(
        functools.partial(mix_kernel, tiles_per),
        grid_spec=pltpu.PrefetchScalarGridSpec(
            num_scalar_prefetch=1,
            grid=(rows // TILE,),
            in_specs=[row, row] + [whole((1, d))] * 3 + [ANY] * (1 + COUNT),
            out_specs=[row, row],
            scratch_shapes=[
                pltpu.VMEM((d, d), bf16),
                pltpu.VMEM((TILE, d), f32),
                pltpu.SemaphoreType.DMA,
            ],
        ),
        out_shape=[jax.ShapeDtypeStruct((rows, d), bf16)] * 2,
        compiler_params=params(1),
        cost_estimate=cost(2 * rows * d * d, rows * d * 12),
        name="mix_norm",
    )(info, mixed, state, b_out, gain, bias, own, *pieces)


def gelu_both(pre):
    sq = pre * pre
    t = jnp.tanh(pre * (GELU_C + GELU_C * GELU_A * sq))
    h = 0.5 + 0.5 * t
    a = pre * h
    return a, h + a * (1.0 - h) * (2.0 * GELU_C + 6.0 * GELU_C * GELU_A * sq)


def ffn_own_kernel(
    info, x, c, w_up, w_down, b_up, grad, acc, g_up, g_down, g_bup, g_bdown, aup, adown, act, gpre
):
    i, tiles = pl.program_id(0), pl.num_programs(0)

    @pl.when(i == 0)
    def _():
        aup[...] = jnp.zeros_like(aup)
        adown[...] = jnp.zeros_like(adown)
        g_bup[...] = jnp.zeros_like(g_bup)
        g_bdown[...] = jnp.zeros_like(g_bdown)

    xs, cs = x[...], c[...]
    a, slope = gelu_both(dot(xs, w_up[...]) + b_up[...])
    gp = dot_nt(cs, w_down[...]) * slope
    act[...] = a.astype(bf16)
    gb = gp.astype(bf16)
    gpre[...] = gb
    grad[...] = dot_nt(gb, w_up[...]).astype(bf16)
    adown[...] += dot_tn(act[...], cs)
    aup[...] += dot_tn(xs, gpre[...])
    g_bup[...] += jnp.sum(gp, axis=0, keepdims=True)
    g_bdown[...] += jnp.sum(cs.astype(f32), axis=0, keepdims=True)

    own = tiles // 4

    @pl.when((i // own) == info[0])
    def _():
        out0 = pl.multiple_of(lax.rem(i, own) * TILE, TILE)
        acc[pl.ds(out0, TILE), :] = dot(act[...], w_down[...])

    @pl.when(i == tiles - 1)
    def _():
        g_up[...] = aup[...].astype(bf16)
        g_down[...] = adown[...].astype(bf16)


def ffn_own_call(info, x, c, w_up, w_down, b_up):
    rows, d = x.shape
    hid = b_up.shape[1]
    row = pl.BlockSpec((TILE, d), lambda i, s: (i, 0))
    return pl.pallas_call(
        ffn_own_kernel,
        grid_spec=pltpu.PrefetchScalarGridSpec(
            num_scalar_prefetch=1,
            grid=(rows // TILE,),
            in_specs=[row, row, once((d, hid)), once((hid, d)), whole((1, hid))],
            out_specs=[
                row, once((rows // 4, d)), once((d, hid)), once((hid, d)), whole((1, hid)),
                whole((1, d)),
            ],
            scratch_shapes=[
                pltpu.VMEM((d, hid), f32),
                pltpu.VMEM((hid, d), f32),
                pltpu.VMEM((TILE, hid), bf16),
                pltpu.VMEM((TILE, hid), bf16),
            ],
        ),
        out_shape=[
            jax.ShapeDtypeStruct((rows, d), bf16),
            jax.ShapeDtypeStruct((rows // 4, d), f32),
            jax.ShapeDtypeStruct((d, hid), bf16),
            jax.ShapeDtypeStruct((hid, d), bf16),
            jax.ShapeDtypeStruct((1, hid), f32),
            jax.ShapeDtypeStruct((1, d), f32),
        ],
        compiler_params=params(1),
        cost_estimate=cost(rows * d * hid * 2 * 5.25, rows * d * 8),
        name="ffn_own",
    )(info, x, c, w_up, w_down, b_up)


def ffn_rest_kernel(
    tiles_per, info, x, c, b_up, state, before, acc_in, gain, b_down, out_own, *rest
):
    ffn_refs, out_refs = rest[:COUNT], rest[COUNT : 2 * COUNT]
    out, half, g_mixed, vecs, w, w_out, grad, acc, act, sems, out_sem = rest[2 * COUNT :]
    k, i = pl.program_id(0), pl.program_id(1)
    blocks, tiles = pl.num_programs(0), pl.num_programs(1)
    hid = w.shape[1] // 2
    piece = hid // GROUP
    slot = lax.rem(k, 2)

    def load(kk, where):
        for ref, m in zip(ffn_refs, PIECES):
            off = pl.multiple_of((info[1] ^ m) * piece, 16)
            for part in range(2):
                pltpu.make_async_copy(
                    ref.at[kk, pl.ds(part * piece, piece)],
                    w.at[where, pl.ds(part * hid + off, piece)],
                    sems.at[where],
                ).start()

    @pl.when((k == 0) & (i == 0))
    def _():
        load(0, 0)
        vecs[...] = jnp.zeros_like(vecs)
        first = (out_own.shape[0] // GROUP) * 2
        start_loads(info, out_refs, out_own, out_targets(w_out, first), out_sem)

    @pl.when(i == 0)
    def _():
        wait_whole(w.at[slot], sems.at[slot])

        @pl.when(k + 1 < blocks)
        def _():
            load(k + 1, 1 - slot)

    @pl.when((k == blocks - 1) & (i == 0))
    def _():
        wait_whole(w_out, out_sem)

    row0 = pl.multiple_of(i * TILE, TILE)
    xs = x[pl.ds(row0, TILE), :]
    cs = c[pl.ds(row0, TILE), :]
    src_t = (info[0] + 3 - k) & 3
    a, slope = gelu_both(dot_nt(xs, w[slot, :hid]) + b_up[pl.ds(src_t, 1), :])
    gb = (dot_nt(cs, w[slot, hid:]) * slope).astype(bf16)
    act[...] = a.astype(bf16)
    part = dot(gb, w[slot, :hid])

    @pl.when(k == 0)
    def _():
        grad[pl.ds(row0, TILE), :] = before[...].astype(f32) + part

    @pl.when((k > 0) & (k < blocks - 1))
    def _():
        grad[pl.ds(row0, TILE), :] += part

    own = tiles // 4
    mine = (i // own) == info[0]
    out0 = pl.multiple_of(lax.rem(i, own) * TILE, TILE)

    @pl.when(mine & (k == 0))
    def _():
        acc[pl.ds(out0, TILE), :] = acc_in[pl.ds(out0, TILE), :] + dot(act[...], w[slot, hid:])

    @pl.when(mine & (k > 0))
    def _():
        acc[pl.ds(out0, TILE), :] += dot(act[...], w[slot, hid:])

    @pl.when(k == blocks - 1)
    def _():
        g2 = grad[pl.ds(row0, TILE), :] + part
        s1 = state[...].astype(f32)
        n, r = normalise(s1)
        g1 = cs.astype(f32) + norm_back(g2, n, r, gain[...])
        half[...] = g1.astype(bf16)
        vecs[0:1, :] += jnp.sum(g2 * n, axis=0, keepdims=True)
        vecs[1:2, :] += jnp.sum(g2, axis=0, keepdims=True)
        vecs[2:3, :] += jnp.sum(g1, axis=0, keepdims=True)

        first, length = tile_length(info, i, tiles_per)

        @pl.when(first < length)
        def _():
            pos = lax.broadcasted_iota(jnp.int32, (TILE, 1), 0) + first
            g_mixed[...] = jnp.where(
                pos < length, dot_nt(half[...], w_out[...]), 0.0
            ).astype(bf16)

        @pl.when(mine)
        def _():
            out[pl.ds(out0, TILE), :] = (
                s1 + acc[pl.ds(out0, TILE), :] + b_down[...]
            ).astype(bf16)


def ffn_rest_call(
    info, x, c, b_up, state, before, acc, gain, b_down, out_own, out_pieces, pieces, tiles_per
):
    rows, d = x.shape
    hid = b_up.shape[1]
    tiles = rows // TILE
    last = pl.BlockSpec((TILE, d), lambda k, i, s: (jnp.where(k == 2, i, 0), 0))
    early = pl.BlockSpec((TILE, d), lambda k, i, s: (jnp.where(k == 0, i, tiles - 1), 0))
    return pl.pallas_call(
        functools.partial(ffn_rest_kernel, tiles_per),
        grid_spec=pltpu.PrefetchScalarGridSpec(
            num_scalar_prefetch=1,
            grid=(3, tiles),
            in_specs=[
                once((rows, d)), once((rows, d)), whole((4, hid)), last, early,
                once((rows // 4, d)), whole((1, d)), whole((1, d)), ANY,
            ]
            + [ANY] * (2 * COUNT),
            out_specs=[once((rows // 4, d)), last, last, whole((8, d))],
            scratch_shapes=[
                pltpu.VMEM((2, 2 * hid, d), bf16),
                pltpu.VMEM((d, d), bf16),
                pltpu.VMEM((rows, d), f32),
                pltpu.VMEM((rows // 4, d), f32),
                pltpu.VMEM((TILE, hid), bf16),
                pltpu.SemaphoreType.DMA((2,)),
                pltpu.SemaphoreType.DMA,
            ],
        ),
        out_shape=[
            jax.ShapeDtypeStruct((rows // 4, d), bf16),
            jax.ShapeDtypeStruct((rows, d), bf16),
            jax.ShapeDtypeStruct((rows, d), bf16),
            jax.ShapeDtypeStruct((8, d), f32),
        ],
        compiler_params=params(2),
        cost_estimate=cost(rows * d * hid * 2 * 11, rows * d * 20),
        name="ffn_rest",
    )(info, x, c, b_up, state, before, acc, gain, b_down, out_own, *pieces, *out_pieces)


def norm_one_kernel(tiles_per, info, dq, dk, dv, state, gs, gain, *rest):
    own, refs, (half, vecs, w, grad, sem) = rest[0], rest[1 : 1 + COUNT], rest[1 + COUNT :]
    i = pl.program_id(0)
    d = dq.shape[1]

    @pl.when(i == 0)
    def _():
        start_loads(info, refs, own, qkv_targets(w), sem)
        vecs[...] = jnp.zeros_like(vecs)
        wait_whole(w, sem)

    first, length = tile_length(info, i, tiles_per)

    @pl.when(first < length)
    def _():
        grad[...] = (
            dot(dq[...], w[:d]) + dot(dk[...], w[d : 2 * d]) + dot(dv[...], w[2 * d :])
        )
        n, r = normalise(state[...].astype(f32))
        g1 = grad[...]
        g0 = gs[...].astype(f32) + norm_back(g1, n, r, gain[...])
        half[...] = g0.astype(bf16)
        vecs[0:1, :] += jnp.sum(g1 * n, axis=0, keepdims=True)
        vecs[1:2, :] += jnp.sum(g1, axis=0, keepdims=True)
        vecs[2:3, :] += jnp.sum(g0, axis=0, keepdims=True)

    @pl.when(first >= length)
    def _():
        half[...] = gs[...]
        vecs[2:3, :] += jnp.sum(gs[...].astype(f32), axis=0, keepdims=True)


def norm_one_call(info, dq, dk, dv, state, gs, gain, own, pieces, tiles_per):
    rows, d = dq.shape
    row = pl.BlockSpec((TILE, d), lambda i, s: (i, 0))
    return pl.pallas_call(
        functools.partial(norm_one_kernel, tiles_per),
        grid_spec=pltpu.PrefetchScalarGridSpec(
            num_scalar_prefetch=1,
            grid=(rows // TILE,),
            in_specs=[row] * 5 + [whole((1, d))] + [ANY] * (1 + COUNT),
            out_specs=[row, whole((8, d))],
            scratch_shapes=[
                pltpu.VMEM((3 * d, d), bf16),
                pltpu.VMEM((TILE, d), f32),
                pltpu.SemaphoreType.DMA,
            ],
        ),
        out_shape=[jax.ShapeDtypeStruct((rows, d), bf16), jax.ShapeDtypeStruct((8, d), f32)],
        compiler_params=params(1),
        cost_estimate=cost(6 * rows * d * d, rows * d * 16),
        name="norm_one_back",
    )(info, dq, dk, dv, state, gs, gain, own, *pieces)


def joined_kernel(info, half, o0, o1, o2, o3, *rest):
    own, refs = rest[0], rest[1 : 1 + COUNT]
    g_hid, g_skp, out, w, sem = rest[1 + COUNT :]
    d = half.shape[1]
    i = pl.program_id(0)

    @pl.when(i == 0)
    def _():
        start_loads(info, refs, own, skip_targets(w), sem)
        wait_whole(w, sem)

    h = half[...]
    g_hid[...] = dot_nt(h, w[:d]).astype(bf16)
    g_skp[...] = dot_nt(h, w[d:]).astype(bf16)
    source = (info[0] + 4 - i // (pl.num_programs(0) // 4)) & 3
    for k, ref in enumerate((o0, o1, o2, o3)):

        @pl.when(source == k)
        def _(ref=ref):
            out[...] = ref[...]


def joined_call(info, half, parts, own, pieces):
    rows, d = half.shape
    row = pl.BlockSpec((TILE, d), lambda i, s: (i, 0))
    per = rows // TILE // 4

    def part_spec(k):
        def index(i, s):
            at = i - ((s[0] + 4 - k) & 3) * per
            return jnp.clip(at, 0, per - 1), 0

        return pl.BlockSpec((TILE, d), index)

    return pl.pallas_call(
        joined_kernel,
        grid_spec=pltpu.PrefetchScalarGridSpec(
            num_scalar_prefetch=1,
            grid=(rows // TILE,),
            in_specs=[row] + [part_spec(k) for k in range(4)] + [ANY] * (1 + COUNT),
            out_specs=[row] * 3,
            scratch_shapes=[pltpu.VMEM((2 * d, d), bf16), pltpu.SemaphoreType.DMA],
        ),
        out_shape=[jax.ShapeDtypeStruct((rows, d), bf16)] * 3,
        compiler_params=params(1),
        cost_estimate=cost(4 * rows * d * d, rows * d * 6),
        name="joined_back",
    )(info, half, *parts, own, *pieces)


def outer(a, b):
    return lax.dot_general(a, b, TN, preferred_element_type=f32).astype(bf16)


def total_over_batch(x):
    n = lax.axis_size("batch")
    if n != GROUP:
        return lax.psum(x, "batch")
    me = lax.axis_index("batch")

    def part(array, index):
        return lax.dynamic_index_in_dim(array, index, 0, keepdims=False)

    total = part(x, me).astype(f32)
    for m in range(1, GROUP):
        total = total + across(part(x, me ^ m), m).astype(f32)
    total = total.astype(bf16)
    sums = jnp.stack([total] + [across(total, m) for m in range(1, GROUP)])
    return jnp.stack([part(sums, me ^ p) for p in range(GROUP)])


def outer(a, b):
    return lax.dot_general(a, b, TN, preferred_element_type=f32).astype(bf16)


def body(
    hidden_in,
    skip_state,
    lengths,
    w_skip,
    b_skip,
    norm1_gain,
    norm1_bias,
    w_qkv,
    b_qv,
    w_out,
    b_out,
    norm2_gain,
    norm2_bias,
    w_up,
    b_up,
    w_down,
    b_down,
    cotangent,
):
    tensor = lax.axis_index("tensor")
    member = lax.rem(lax.axis_index("batch"), GROUP)
    info = jnp.concatenate([jnp.stack([tensor, member]).astype(jnp.int32), lengths])
    rows, d = hidden_in.shape
    seq = rows // lengths.shape[0]
    tiles_per = seq // TILE
    columns = w_out.shape[0]

    def share(array, axis=0):
        size = array.shape[axis] // GROUP
        return lax.dynamic_slice_in_dim(array, member * size, size, axis)

    biases = jnp.concatenate([b_qv.reshape(-1), b_up])
    b_hi = biases.astype(bf16)
    b_mid = (biases - b_hi.astype(f32)).astype(bf16)
    b_low = (biases - b_hi.astype(f32) - b_mid.astype(f32)).astype(bf16)
    b_rows = jnp.concatenate([b_hi, b_mid, b_low])
    b_rows = jnp.pad(b_rows, (0, 16 * d - b_rows.size)).reshape(16, d)

    qkv_own = jnp.swapaxes(w_qkv, 1, 2)
    first_piece = jnp.concatenate([share(w_skip), share(w_out)], 0)
    qkv_piece = share(qkv_own, 1).reshape(-1, d)
    qkv_rows = qkv_piece.shape[0]
    qkv_piece = jnp.concatenate([qkv_piece, b_rows], 0)
    qkv_own = qkv_own.reshape(-1, d)
    up_piece = jnp.swapaxes(share(w_up, 1), 0, 1)
    ffn_piece = jnp.concatenate([up_piece, share(w_down)], 0)

    first_z = jnp.stack([along(first_piece, k) for k in (1, 2, 3)])
    qkv_z = [along(after(qkv_piece, first_z), k) for k in (1, 2, 3)]
    first_chips = from_chips(first_z)
    terms = jnp.stack([b_rows] + [x[qkv_rows:] for x in qkv_z]).reshape(4, -1).astype(f32)
    size = biases.size
    relative = terms[:, :size] + terms[:, size : 2 * size] + terms[:, 2 * size : 3 * size]
    all_biases = jnp.stack([relative[(tensor - j) & 3] for j in range(4)])
    b_q = all_biases[:, :columns].reshape(1, d)
    b_v = all_biases[:, columns : 2 * columns].reshape(1, d)
    b_up_all = all_biases[:, 2 * columns :]
    qkv_z = jnp.stack([x[:qkv_rows] for x in qkv_z])
    first_all = from_cores(first_chips)
    qkv_chips = from_chips(after(qkv_z, *first_chips))
    ffn_piece = after(ffn_piece, qkv_z)
    ffn_z = [along(ffn_piece, k) for k in (1, 2, 3)]
    def line(v):
        return v[None, :]

    state_zero, normed_one = skip_call(
        info, hidden_in, skip_state, line(b_skip), line(norm1_gain), line(norm1_bias),
        w_skip, first_all,
    )
    qkv_all = from_cores(list(lax.optimization_barrier((tuple(qkv_chips), normed_one))[0]))
    q, k, v = qkv_call(info, normed_one, b_q, b_v, qkv_own, qkv_all, tiles_per)
    ffn_z = jnp.stack(ffn_z)
    ffn_chips = from_chips(after(ffn_z, q))
    mixed, lse = attend_call(info, q, k, v, seq)
    lse = lse[:, :HEADS].T
    state_one, normed_two = mix_call(
        info, mixed, state_zero, line(b_out), line(norm2_gain), line(norm2_bias), w_out, first_all,
        tiles_per,
    )
    before, acc, g_up, g_down, g_bup, g_bdown = ffn_own_call(
        info, normed_two, cotangent, w_up, w_down, line(b_up)
    )
    ffn_all = from_cores(list(lax.optimization_barrier((tuple(ffn_chips), before))[0]))
    out_rows, half_one, grad_mixed, vecs_two = ffn_rest_call(
        info, normed_two, cotangent, b_up_all, state_one, before, acc, line(norm2_gain),
        line(b_down), w_out, first_all, ffn_all, tiles_per,
    )
    out_parts = [out_rows] + [along(out_rows, k) for k in (1, 2, 3)]
    g_up, g_down = lax.psum((g_up, g_down), "batch")

    first_col = tensor * columns

    def own(array):
        return lax.dynamic_slice_in_dim(array, first_col, columns, 1)

    g_out = outer(own(mixed), half_one)
    dq, dk, dv = attend_back_call(info, q, k, v, grad_mixed, mixed, lse, seq)
    half_zero, vecs_one = norm_one_call(
        info, dq, dk, dv, state_zero, half_one, line(norm1_gain), qkv_own, qkv_all, tiles_per
    )
    g_qkv = jnp.stack([outer(normed_one, own(x)) for x in (dq, dk, dv)])
    shard = w_skip.shape[0]
    joined = jnp.concatenate([hidden_in, skip_state], axis=1)
    features = lax.dynamic_slice_in_dim(joined, tensor * shard, shard, 1)
    g_skip = outer(features, half_zero)
    g_bqv = jnp.stack([jnp.sum(own(x), axis=0, dtype=f32) for x in (dq, dv)]).reshape(1, -1)
    g_bqv = jnp.pad(g_bqv, ((0, 0), (0, d - g_bqv.shape[1])))
    vectors = jnp.concatenate(
        [vecs_two[:3], g_bdown, vecs_one[:3], g_bqv, g_bup.reshape(-1, d)], axis=0
    )
    vectors = jnp.pad(vectors, ((0, 2 * GROUP - vectors.shape[0]), (0, 0))).astype(bf16)
    tied = lax.optimization_barrier((g_qkv, g_out, g_up, g_down))
    g_qkv, g_out = lax.psum((tied[0], tied[1]), "batch")
    g_up, g_down = tied[2], tied[3]
    last = jnp.concatenate([g_skip.reshape(GROUP, -1, d), vectors.reshape(GROUP, 2, d)], axis=1)
    last = total_over_batch(last).astype(f32)
    g_skip = last[:, :-2].reshape(-1, d)
    vectors = last[:, -2:].reshape(-1, d)
    grad_hidden, grad_skip, output = joined_call(info, half_zero, out_parts, w_skip, first_all)
    return (
        output,
        grad_hidden,
        grad_skip,
        g_skip,
        vectors[6],
        vectors[4],
        vectors[5],
        g_qkv.astype(f32),
        vectors[7, : 2 * columns].reshape(2, columns),
        g_out.astype(f32),
        vectors[2],
        vectors[0],
        vectors[1],
        g_up.astype(f32),
        vectors[8 : 8 + g_bup.size // d].reshape(-1),
        g_down.astype(f32),
        vectors[3],
    )


def solution(mesh):
    placed = (
        P("batch", None),
        P("batch", None),
        P("batch"),
        P("tensor", None),
        P(),
        P(),
        P(),
        P(None, None, "tensor"),
        P(None, "tensor"),
        P("tensor", None),
        P(),
        P(),
        P(),
        P(None, "tensor"),
        P("tensor"),
        P("tensor", None),
        P(),
        P("batch", None),
    )
    return jax.shard_map(
        body,
        mesh=mesh,
        in_specs=placed,
        out_specs=(
            P("batch", None),
            P("batch", None),
            P("batch", None),
            P("tensor", None),
            P(),
            P(),
            P(),
            P(None, None, "tensor"),
            P(None, "tensor"),
            P("tensor", None),
            P(),
            P(),
            P(),
            P(None, "tensor"),
            P("tensor"),
            P("tensor", None),
            P(),
        ),
        check_vma=False,
    )
```

time: 1110 us -> 576 us (0.52)
  waiting for transfers between devices: 676 us -> 132 us
  Pallas kernels: 0 us -> 245 us
  matrix products: 189 us -> 16.4 us
  starting transfers between devices: 0.2 us -> 125 us
  other arithmetic: 99.8 us -> 16.8 us
  local copies, waits for them, and re-layouts: 98.5 us -> 19.7 us
  blocking collectives: 25.9 us -> 0 us
    psum x4 -> x2, waiting for transfers between devices: 591 us -> 22.4 us  [the longest x1 22.4 us: body(): g_qkv, g_out = lax.psum((tied[0], tied[1]), 'batch')]
    pallas_call x0 -> x9, Pallas kernels: none -> 245 us  [the longest x1 72.1 us: ffn_rest_call(): pl.pallas_call(functools.partial(ffn_rest_kernel, tiles_per), grid_spec=p...]
    dot_general x46 -> x5, matrix products: 189 us -> 16.4 us  [outer(): return lax.dot_general(a, b, TN, preferred_element_type=f32).astype(bf16)]
    ppermute x0 -> x47, starting transfers between devices: none -> 125 us  [the longest x35 110 us: across(): return lax.ppermute(x, 'batch', [(i, i ^ m) for i in range(n)])]
    ppermute x0 -> x47, waiting for transfers between devices: none -> 109 us  [the longest x35 65.3 us: across(): return lax.ppermute(x, 'batch', [(i, i ^ m) for i in range(n)])]
    all_gather x1 -> x0, waiting for transfers between devices: 84.2 us -> none  [body(): whole_skip = lax.all_gather(w_skip, 'tensor', axis=0, tiled=True)]
    reduce_sum x15 -> x1, other arithmetic: 53.1 us -> 1.87 us  [body(): jnp.sum(own(x), axis=0, dtype=f32)]
    convert_element_type x33 -> x5, other arithmetic: 40 us -> 10.9 us  [the longest x1 4.22 us: body(): g_up.astype(f32)]
  transfers between devices with their start and end apart: 5 -> 49, of which waited for: 5 -> 21; matrix products, arithmetic and copies ran while one was open for 9% -> 8% of each run, Pallas kernels for 0% -> 37%
where the time goes in v1:
time: 576 us; the launch traced here: 570 us
  Pallas kernels  245 us (43%)
  waiting for transfers between devices  132 us (23%)
  starting transfers between devices  125 us (22%)
  local copies, waits for them, and re-layouts  19.7 us (3%)
  other arithmetic  16.8 us (3%)
  matrix products  16.4 us (3%)
  between operations  15 us (3%)
    ppermute x35, starting transfers between devices, across(): return lax.ppermute(x, 'batch', [(i, i ^ m) for i in range(n)])  110 us
    pallas_call x1, Pallas kernels, ffn_rest_call(): pl.pallas_call(functools.partial(ffn_rest_kernel, tiles_per), grid_spec=p...  72.1 us
    ppermute x35, waiting for transfers between devices, across(): return lax.ppermute(x, 'batch', [(i, i ^ m) for i in range(n)])  65.3 us
    ppermute x12, waiting for transfers between devices, along(): return lax.ppermute(x, 'tensor', [(i, (i + k) % n) for i in range(n)])  43.8 us
    pallas_call x1, Pallas kernels, ffn_own_call(): pl.pallas_call(ffn_own_kernel, grid_spec=pltpu.PrefetchScalarGridSpec(num...  34.3 us
    pallas_call x1, Pallas kernels, attend_back_call(): pl.pallas_call(attend_back_kernel, grid_spec=pltpu.PrefetchScalarGridSpec...  29.7 us
    pallas_call x1, Pallas kernels, attend_call(): pl.pallas_call(attend_kernel, grid_spec=pltpu.PrefetchScalarGridSpec(num_...  23.6 us
    psum x1, waiting for transfers between devices, body(): g_qkv, g_out = lax.psum((tied[0], tied[1]), 'batch')  22.4 us
  transfers between devices with their start and end apart: 49, of which 21 were waited for; matrix products, arithmetic and copies ran while one was open for 8% of the time, Pallas kernels for 37%

profile of v1, /device:TPU:0, one launch (start us, length us, event | category | flops | bytes accessed | tf_op | source)
XLA Modules:
  0.0 569.6 jit_solution(15982301866362624911)
XLA Ops:
  7.3 1.0 constant_dynamic-slice_fusion.6
  8.2 0.9 constant_dynamic-slice_fusion.7
  9.8 5.0 collective-permute-start.2
  14.9 1.0 collective-permute-start
  17.4 1.0 constant_dynamic-slice_fusion.1
  19.1 1.8 copy.36
  20.8 1.0 constant_dynamic-slice_fusion
  21.8 9.9 %collective-permute-done.1 = bf16[96,1024]{1,0:T(8,128)(2,1)S(1)} collective-permute-done((bf16[96,1024]{1,0:T(8,128)(2,1)}, bf16[96,1024]{1,0:T(8,128)(2,1)S(1)}, u32[]{:S(2)}, u32[]{:S(2)}) %collective-permute-start.1) | collective-permute-done | bytes 196640 | tf_op jit(solution)/shard_map/ppermute | solution.py:55
  33.0 2.5 collective-permute-start.5
  36.6 2.0 collective-permute-done.12
  38.6 2.9 collective-permute-start.11
  41.5 9.0 %collective-permute-done.11 = bf16[112,1024]{1,0:T(8,128)(2,1)S(1)} collective-permute-done((bf16[112,1024]{1,0:T(8,128)(2,1)S(1)}, bf16[112,1024]{1,0:T(8,128)(2,1)S(1)}, u32[]{:S(2)}, u32[]{:S(2)}) %collective-permute-start.11) | collective-permute-done | bytes 229408 | tf_op jit(solution)/shard_map/ppermute | solution.py:55
  50.9 11.4 %collective-permute-done.4.rest_3_.rest_10_ = bf16[3,96,1024]{2,1,0:T(8,128)(2,1)S(1)} collective-permute-done((bf16[3,96,1024]{2,1,0:T(8,128)(2,1)S(1)}, bf16[3,96,1024]{2,1,0:T(8,128)(2,1)S(1)}, u32[]{:S(2)}, u32[]{:S(2)}) %collective-permute-start.4) | collective-permute-done | bytes 589856 | tf_op jit(solution)/shard_map/ppermute | solution.py:60
  63.1 3.9 collective-permute-start.22
  67.1 1.8 collective-permute-start.15
  68.9 1.2 collective-permute-start.14
  71.0 17.5 %skip_norm.1 = (bf16[2048,1024]{1,0:T(8,128)(2,1)}, bf16[2048,1024]{1,0:T(8,128)(2,1)}) custom-call(s32[4]{0:T(128)} %pad_add_fusion.info, bf16[2048,1024]{1,0:T(8,128)(2,1)} %hid.1, bf16[2048,1024]{1,0:T(8,128)(2,1)} %skp.1, f32[1,1024]{1,0:T(1,128)} %bitcast.143, f32[1,1024]{1,0:T(1,128)} %bitcast.150, f32[1,1024]{1,0:T(1,128)} %bitcast.144, ...), custom_call_target="tpu_custom_call" | custom-call | flops 8589934592 | bytes 25165824 | tf_op jit(solution)/shard_map/skip_norm/pallas_call | solution.py:158
  89.1 6.8 %collective-permute-done.14.rest_3_ = bf16[3,96,1024]{2,1,0:T(8,128)(2,1)} collective-permute-done((bf16[3,96,1024]{2,1,0:T(8,128)(2,1)S(1)}, bf16[3,96,1024]{2,1,0:T(8,128)(2,1)}, u32[]{:S(2)}, u32[]{:S(2)}) %collective-permute-start.14) | collective-permute-done | bytes 589856 | tf_op jit(solution)/shard_map/ppermute | solution.py:60
  96.5 15.4 %collective-permute-done.21 = bf16[256,1024]{1,0:T(8,128)(2,1)S(1)} collective-permute-done((bf16[256,1024]{1,0:T(8,128)(2,1)S(1)}, bf16[256,1024]{1,0:T(8,128)(2,1)S(1)}, u32[]{:S(2)}, u32[]{:S(2)}) %collective-permute-start.21) | collective-permute-done | bytes 524320 | tf_op jit(solution)/shard_map/ppermute | solution.py:55
  114.3 0.9 copy-done.18
  116.8 15.9 %qkv.1 = (bf16[2048,1024]{1,0:T(8,128)(2,1)}, bf16[2048,1024]{1,0:T(8,128)(2,1)}, bf16[2048,1024]{1,0:T(8,128)(2,1)}) custom-call(s32[4]{0:T(128)} %pad_add_fusion.info, bf16[2048,1024]{1,0:T(8,128)(2,1)} %get-tuple-element.60.x, f32[1,1024]{1,0:T(1,128)} %bitcast.141, f32[1,1024]{1,0:T(1,128)} %bitcast.140, bf16[768,1024]{1,0:T(8,128)(2,1)} %bitcast.116, ...), custom_call_target="tpu_custom_call" | custom-call | flops 8589934592 | bytes 23068672 | tf_op jit(solution)/shard_map/qkv/pallas_call | solution.py:207
  133.4 4.9 collective-permute-start.24
  138.3 23.6 %attend.1 = (bf16[2048,1024]{1,0:T(8,128)(2,1)}, f32[2048,128]{1,0:T(8,128)}) custom-call(s32[4]{0:T(128)} %pad_add_fusion.info, bf16[2048,1024]{1,0:T(8,128)(2,1)} %get-tuple-element.67.q, bf16[2048,1024]{1,0:T(8,128)(2,1)} %get-tuple-element.68.k, bf16[2048,1024]{1,0:T(8,128)(2,1)} %get-tuple-element.69.v), custom_call_target="tpu_custom_call" | custom-call | flops 8589934592 | bytes 16777216 | tf_op jit(solution)/shard_map/attend/pallas_call | solution.py:284
  161.9 13.8 %mix_norm.1 = (bf16[2048,1024]{1,0:T(8,128)(2,1)}, bf16[2048,1024]{1,0:T(8,128)(2,1)}) custom-call(s32[4]{0:T(128)} %pad_add_fusion.info, bf16[2048,1024]{1,0:T(8,128)(2,1)} %get-tuple-element.70.mixed.o, bf16[2048,1024]{1,0:T(8,128)(2,1)} %get-tuple-element.71.state, f32[1,1024]{1,0:T(1,128)} %bitcast.145, f32[1,1024]{1,0:T(1,128)} %bitcast.147, ...), custom_call_target="tpu_custom_call" | custom-call | flops 4294967296 | bytes 25165824 | tf_op jit(solution)/shard_map/mix_norm/pallas_call | solution.py:421
  175.8 34.3 %ffn_own.1 = (bf16[2048,1024]{1,0:T(8,128)(2,1)}, f32[512,1024]{1,0:T(8,128)}, bf16[1024,1024]{1,0:T(8,128)(2,1)}, bf16[1024,1024]{1,0:T(8,128)(2,1)}, f32[1,1024]{1,0:T(1,128)}, /*index=5*/f32[1,1024]{1,0:T(1,128)}) custom-call(s32[4]{0:T(128)} %pad_add_fusion.info, bf16[2048,1024]{1,0:T(8,128)(2,1)} %get-tuple-element.72.x, bf16[2048,1024]{1,0:T(8,128)(2,1)} %c.3, ...), custom_call_target="tpu_custom_call" | custom-call | flops 22548578304 | bytes 16777216 | tf_op jit(solution)/shard_map/ffn_own/pallas_call | solution.py:490
  210.1 32.8 %collective-permute-start.26 = (bf16[3,256,1024]{2,1,0:T(8,128)(2,1)S(1)}, bf16[3,256,1024]{2,1,0:T(8,128)(2,1)}, u32[]{:S(2)}, u32[]{:S(2)}) collective-permute-start(bf16[3,256,1024]{2,1,0:T(8,128)(2,1)S(1)} %pad_maximum_fusion.rest_0_), channel_id=1, source_target_pairs={{0,4},{4,0},{8,12},{12,8},{16,20},{20,16},{24,28},{28,24},{1,5},{5... | collective-permute-start | bytes 4718600 | tf_op jit(solution)/shard_map/ppermute | solution.py:60
  244.1 1.6 copy.38
  246.4 1.1 collective-permute-done.26.rest_4_
  247.5 1.0 collective-permute-done.27.rest_5_
  248.5 2.2 collective-permute-done.28.rest_6_
  250.8 3.0 collective-permute-done.29.rest_7_
  253.8 72.1 %ffn_rest.1 = (bf16[512,1024]{1,0:T(8,128)(2,1)}, bf16[2048,1024]{1,0:T(8,128)(2,1)}, bf16[2048,1024]{1,0:T(8,128)(2,1)}, f32[8,1024]{1,0:T(8,128)}) custom-call(s32[4]{0:T(128)} %pad_add_fusion.info, bf16[2048,1024]{1,0:T(8,128)(2,1)} %get-tuple-element.72.x, bf16[2048,1024]{1,0:T(8,128)(2,1)} %c.3, f32[4,1024]{1,0:T(4,128)} %pad_maximum_fusion.7.b_up, ...), custom_call_target="tpu_custom_call" | custom-call | flops 47244640256 | bytes 41943040 | tf_op jit(solution)/shard_map/ffn_rest/pallas_call | solution.py:625
  325.8 29.7 %attend_back.1 = (bf16[2048,1024]{1,0:T(8,128)(2,1)}, bf16[2048,1024]{1,0:T(8,128)(2,1)}, bf16[2048,1024]{1,0:T(8,128)(2,1)}) custom-call(s32[4]{0:T(128)} %pad_add_fusion.info, bf16[2048,1024]{1,0:T(8,128)(2,1)} %get-tuple-element.67.q, bf16[2048,1024]{1,0:T(8,128)(2,1)} %get-tuple-element.68.k, bf16[2048,1024]{1,0:T(8,128)(2,1)} %get-tuple-element.69.v, ...), custom_call_target="tpu_custom_call" | custom-call | flops 21474836480 | bytes 33554432 | tf_op jit(solution)/shard_map/attend_back/pallas_call | solution.py:375
  355.6 20.1 %norm_one_back.1 = (bf16[2048,1024]{1,0:T(8,128)(2,1)}, f32[8,1024]{1,0:T(8,128)}) custom-call(s32[4]{0:T(128)} %pad_add_fusion.info, bf16[2048,1024]{1,0:T(8,128)(2,1)} %get-tuple-element.84.dq, bf16[2048,1024]{1,0:T(8,128)(2,1)} %get-tuple-element.85.dk, bf16[2048,1024]{1,0:T(8,128)(2,1)} %get-tuple-element.86.dv, ...), custom_call_target="tpu_custom_call" | custom-call | flops 12884901888 | bytes 33554432 | tf_op jit(solution)/shard_map/norm_one_back/pallas_call | solution.py:693
  376.4 1.9 dynamic-slice_reduce_fusion
  379.2 5.4 fusion.3
  384.8 50.4 %collective-permute-start.33 = (bf16[66,1024]{1,0:T(8,128)(2,1)S(1)}, bf16[66,1024]{1,0:T(8,128)(2,1)S(1)}, u32[]{:S(2)}, u32[]{:S(2)}) collective-permute-start(bf16[66,1024]{1,0:T(8,128)(2,1)S(1)} %get-tuple-element.109), channel_id=1, source_target_pairs={{0,4},{4,0},{8,12},{12,8},{16,20},{20,16},{24,28},{28,24},{1,5},{5... | collective-permute-start | bytes 405512 | tf_op jit(solution)/shard_map/ppermute | solution.py:60
  435.2 2.5 fusion.7
  437.8 2.5 fusion.6
  440.3 2.7 fusion.8
  443.0 1.9 collective-permute-start.34
  445.1 2.7 collective-permute-start.36
  448.2 1.2 collective-permute-start.38
  449.5 3.3 convolution_convert_fusion
  452.8 0.9 collective-permute-start.31
  453.7 1.4 collective-permute-done.36
  455.6 3.2 collective-permute-done.37
  459.3 1.3 pad_maximum_fusion.1
  460.6 4.2 convert_element_type.118
  464.8 2.5 convert_element_type.119
  467.3 1.5 collective-permute-start.45
  468.8 1.9 collective-permute-start.41
  470.8 12.7 %collective-permute-done.41 = bf16[66,1024]{1,0:T(8,128)(2,1)S(1)} collective-permute-done((bf16[66,1024]{1,0:T(8,128)(2,1)S(1)}, bf16[66,1024]{1,0:T(8,128)(2,1)S(1)}, u32[]{:S(2)}, u32[]{:S(2)}) %collective-permute-start.41) | collective-permute-done | bytes 135200 | tf_op jit(solution)/shard_map/ppermute | solution.py:60
  483.5 5.8 %collective-permute-done.42 = bf16[66,1024]{1,0:T(8,128)(2,1)S(1)} collective-permute-done((bf16[66,1024]{1,0:T(8,128)(2,1)S(1)}, bf16[66,1024]{1,0:T(8,128)(2,1)S(1)}, u32[]{:S(2)}, u32[]{:S(2)}) %collective-permute-start.42) | collective-permute-done | bytes 135200 | tf_op jit(solution)/shard_map/ppermute | solution.py:60
  489.8 5.0 collective-permute-done.43
  494.8 6.1 %collective-permute-done.44 = bf16[66,1024]{1,0:T(8,128)(2,1)S(1)} collective-permute-done((bf16[66,1024]{1,0:T(8,128)(2,1)S(1)}, bf16[66,1024]{1,0:T(8,128)(2,1)S(1)}, u32[]{:S(2)}, u32[]{:S(2)}) %collective-permute-start.44) | collective-permute-done | bytes 135200 | tf_op jit(solution)/shard_map/ppermute | solution.py:60
  500.8 1.4 collective-permute-start.46
  502.3 5.3 collective-permute-done.46
  507.9 1.6 slice.115
  510.8 22.4 %all-reduce.8.cloned.1.call-done = (bf16[3,1024,256]{2,1,0:T(8,128)(2,1)}, bf16[256,1024]{1,0:T(8,128)(2,1)}) async-done(((bf16[3,1024,256]{2,1,0:T(8,128)(2,1)}, bf16[256,1024]{1,0:T(8,128)(2,1)}), (bf16[3,1024,256]{2,1,0:T(8,128)(2,1)}, bf16[256,1024]{1,0:T(8,128)(2,1)})) %all-reduce.8.cloned.1.call-update) | async-done | bytes 2097168 | tf_op jit(solution)/shard_map/psum | solution.py:901
  533.2 2.2 convert_element_type.117
  535.4 1.9 convert_element_type.116
  537.3 7.4 %collective-permute-done.31.o2 = bf16[512,1024]{1,0:T(8,128)(2,1)} collective-permute-done((bf16[512,1024]{1,0:T(8,128)(2,1)S(1)}, bf16[512,1024]{1,0:T(8,128)(2,1)}, u32[]{:S(2)}, u32[]{:S(2)}) %collective-permute-start.31) | collective-permute-done | bytes 1048608 | tf_op jit(solution)/shard_map/ppermute | solution.py:55
  544.8 17.8 %joined_back.1 = (bf16[2048,1024]{1,0:T(8,128)(2,1)}, bf16[2048,1024]{1,0:T(8,128)(2,1)}, bf16[2048,1024]{1,0:T(8,128)(2,1)}) custom-call(s32[4]{0:T(128)} %pad_add_fusion.info, bf16[2048,1024]{1,0:T(8,128)(2,1)} %get-tuple-element.88.half, bf16[512,1024]{1,0:T(8,128)(2,1)} %get-tuple-element.89.o0, bf16[512,1024]{1,0:T(8,128)(2,1)} %collective-permute-done.30.o1, ...), custom_call_target="tpu_custom_call" | custom-call | flops 8589934592 | bytes 12582912 | tf_op jit(solution)/shard_map/joined_back/pallas_call | solution.py:747
  (178 shorter events, 20.5 us)
Async XLA Ops:
  7.2 11.3 %copy-start = (bf16[3,1024,256]{2,1,0:T(8,128)(2,1)S(1)}, bf16[3,1024,256]{2,1,0:T(8,128)(2,1)}, u32[]{:S(2)}) copy-start(bf16[3,1024,256]{2,1,0:T(8,128)(2,1)} %param.25) | copy-start | bytes 4718596
  7.2 453.4 %all-reduce.10.cloned.1.call-start = ((), (), s32[]{:S(2)}) async-start(), calls=%async_computation.1 | async-start | bytes 8388608 | tf_op jit(solution)/shard_map/psum | solution.py:877
  9.8 12.0 %collective-permute-start.2 = (bf16[96,1024]{1,0:T(8,128)(2,1)}, bf16[96,1024]{1,0:T(8,128)(2,1)S(1)}, u32[]{:S(2)}, u32[]{:S(2)}) collective-permute-start(bf16[96,1024]{1,0:T(8,128)(2,1)} %pad_maximum_fusion.6), channel_id=1, source_target_pairs={{0,3},{1,0},{2,1},{3,2},{4,7},{5,4},{6,5},{7,6},{8,11},{9,8},{10,9... | collective-permute-start | bytes 589832 | tf_op jit(solution)/shard_map/ppermute | solution.py:55
  14.9 16.9 %collective-permute-start.1 = (bf16[96,1024]{1,0:T(8,128)(2,1)}, bf16[96,1024]{1,0:T(8,128)(2,1)S(1)}, u32[]{:S(2)}, u32[]{:S(2)}) collective-permute-start(bf16[96,1024]{1,0:T(8,128)(2,1)} %pad_maximum_fusion.6), channel_id=1, source_target_pairs={{0,2},{1,3},{2,0},{3,1},{4,6},{5,7},{6,4},{7,5},{8,10},{9,11},{10,... | collective-permute-start | bytes 589832 | tf_op jit(solution)/shard_map/ppermute | solution.py:55
  14.9 16.9 %collective-permute-start = (bf16[96,1024]{1,0:T(8,128)(2,1)}, bf16[96,1024]{1,0:T(8,128)(2,1)S(1)}, u32[]{:S(2)}, u32[]{:S(2)}) collective-permute-start(bf16[96,1024]{1,0:T(8,128)(2,1)} %pad_maximum_fusion.6), channel_id=1, source_target_pairs={{0,1},{1,2},{2,3},{3,0},{4,5},{5,6},{6,7},{7,4},{8,9},{9,10},{10,1... | collective-permute-start | bytes 589832 | tf_op jit(solution)/shard_map/ppermute | solution.py:55
  20.8 11.5 %copy-start.8 = (s32[2]{0:T(128)S(1)}, s32[2]{0:T(128)}, u32[]{:S(2)}) copy-start(s32[2]{0:T(128)} %param.20) | copy-start | bytes 28
  31.9 31.2 %copy-start.4 = (bf16[3,96,1024]{2,1,0:T(8,128)(2,1)}, bf16[3,96,1024]{2,1,0:T(8,128)(2,1)S(1)}, u32[]{:S(2)}) copy-start(bf16[3,96,1024]{2,1,0:T(8,128)(2,1)S(1)} %pad_maximum_fusion.2.rest_1_.rest_8_) | copy-start | bytes 1769476
  31.9 6.7 %collective-permute-start.12 = (bf16[112,1024]{1,0:T(8,128)(2,1)S(1)}, bf16[112,1024]{1,0:T(8,128)(2,1)S(1)}, u32[]{:S(2)}, u32[]{:S(2)}) collective-permute-start(bf16[112,1024]{1,0:T(8,128)(2,1)S(1)} %pad_maximum_fusion.5), channel_id=1, source_target_pairs={{0,3},{1,0},{2,1},{3,2},{4,7},{5,4},{6,5},{7,6},{8,11},{9,8},{10,9... | collective-permute-start | bytes 688136 | tf_op jit(solution)/shard_map/ppermute | solution.py:55
  32.9 34.2 %collective-permute-start.6 = (bf16[3,96,1024]{2,1,0:T(8,128)(2,1)S(1)}, bf16[3,96,1024]{2,1,0:T(8,128)(2,1)S(1)}, u32[]{:S(2)}, u32[]{:S(2)}) collective-permute-start(bf16[3,96,1024]{2,1,0:T(8,128)(2,1)S(1)} %pad_maximum_fusion.2.rest_1_.rest_8_), channel_id=1, source_target_pairs={{0,4},{4,0},{8,12},{12,8},{16,20},{20,16},{24,28},{28,24},{1,5},{5... | collective-permute-start | bytes 1769480 | tf_op jit(solution)/shard_map/ppermute | solution.py:60
  33.0 17.8 %collective-permute-start.5 = (bf16[3,96,1024]{2,1,0:T(8,128)(2,1)S(1)}, bf16[3,96,1024]{2,1,0:T(8,128)(2,1)S(1)}, u32[]{:S(2)}, u32[]{:S(2)}) collective-permute-start(bf16[3,96,1024]{2,1,0:T(8,128)(2,1)S(1)} %pad_maximum_fusion.2.rest_1_.rest_8_), channel_id=1, source_target_pairs={{0,24},{4,28},{8,16},{12,20},{16,8},{20,12},{24,0},{28,4},{1,25},{... | collective-permute-start | bytes 1769480 | tf_op jit(solution)/shard_map/ppermute | solution.py:60
  35.5 26.8 %collective-permute-start.4 = (bf16[3,96,1024]{2,1,0:T(8,128)(2,1)S(1)}, bf16[3,96,1024]{2,1,0:T(8,128)(2,1)S(1)}, u32[]{:S(2)}, u32[]{:S(2)}) collective-permute-start(bf16[3,96,1024]{2,1,0:T(8,128)(2,1)S(1)} %pad_maximum_fusion.2.rest_1_.rest_8_), channel_id=1, source_target_pairs={{0,16},{4,20},{8,24},{12,28},{16,0},{20,4},{24,8},{28,12},{1,17},{... | collective-permute-start | bytes 1769480 | tf_op jit(solution)/shard_map/ppermute | solution.py:60
  36.0 26.4 %collective-permute-start.3 = (bf16[3,96,1024]{2,1,0:T(8,128)(2,1)S(1)}, bf16[3,96,1024]{2,1,0:T(8,128)(2,1)S(1)}, u32[]{:S(2)}, u32[]{:S(2)}) collective-permute-start(bf16[3,96,1024]{2,1,0:T(8,128)(2,1)S(1)} %pad_maximum_fusion.2.rest_1_.rest_8_), channel_id=1, source_target_pairs={{0,8},{4,12},{8,0},{12,4},{16,24},{20,28},{24,16},{28,20},{1,9},{5... | collective-permute-start | bytes 1769480 | tf_op jit(solution)/shard_map/ppermute | solution.py:60
  38.6 11.8 %collective-permute-start.11 = (bf16[112,1024]{1,0:T(8,128)(2,1)S(1)}, bf16[112,1024]{1,0:T(8,128)(2,1)S(1)}, u32[]{:S(2)}, u32[]{:S(2)}) collective-permute-start(bf16[112,1024]{1,0:T(8,128)(2,1)S(1)} %pad_maximum_fusion.5), channel_id=1, source_target_pairs={{0,2},{1,3},{2,0},{3,1},{4,6},{5,7},{6,4},{7,5},{8,10},{9,11},{10,... | collective-permute-start | bytes 688136 | tf_op jit(solution)/shard_map/ppermute | solution.py:55
  50.4 12.5 %collective-permute-start.10 = (bf16[112,1024]{1,0:T(8,128)(2,1)S(1)}, bf16[112,1024]{1,0:T(8,128)(2,1)S(1)}, u32[]{:S(2)}, u32[]{:S(2)}) collective-permute-start(bf16[112,1024]{1,0:T(8,128)(2,1)S(1)} %pad_maximum_fusion.5), channel_id=1, source_target_pairs={{0,1},{1,2},{2,3},{3,0},{4,5},{5,6},{6,7},{7,4},{8,9},{9,10},{10,1... | collective-permute-start | bytes 688136 | tf_op jit(solution)/shard_map/ppermute | solution.py:55
  50.8 19.3 %copy-start.11 = (bf16[3,96,1024]{2,1,0:T(8,128)(2,1)}, bf16[3,96,1024]{2,1,0:T(8,128)(2,1)S(1)}, u32[]{:S(2)}) copy-start(bf16[3,96,1024]{2,1,0:T(8,128)(2,1)S(1)} %collective-permute-done.5.rest_4_.rest_11_) | copy-start | bytes 1769476
  50.8 16.3 %collective-permute-start.9 = (bf16[3,96,1024]{2,1,0:T(8,128)(2,1)S(1)}, bf16[3,96,1024]{2,1,0:T(8,128)(2,1)S(1)}, u32[]{:S(2)}, u32[]{:S(2)}) collective-permute-start(bf16[3,96,1024]{2,1,0:T(8,128)(2,1)S(1)} %collective-permute-done.5.rest_4_.rest_11_), channel_id=1, source_target_pairs={{0,4},{4,0},{8,12},{12,8},{16,20},{20,16},{24,28},{28,24},{1,5},{5... | collective-permute-start | bytes 1769480 | tf_op jit(solution)/shard_map/ppermute | solution.py:60
  62.3 8.5 %copy-start.12 = (bf16[3,96,1024]{2,1,0:T(8,128)(2,1)}, bf16[3,96,1024]{2,1,0:T(8,128)(2,1)S(1)}, u32[]{:S(2)}) copy-start(bf16[3,96,1024]{2,1,0:T(8,128)(2,1)S(1)} %collective-permute-done.4.rest_3_.rest_10_) | copy-start | bytes 1769476
  62.3 6.6 %collective-permute-start.8 = (bf16[3,96,1024]{2,1,0:T(8,128)(2,1)S(1)}, bf16[3,96,1024]{2,1,0:T(8,128)(2,1)S(1)}, u32[]{:S(2)}, u32[]{:S(2)}) collective-permute-start(bf16[3,96,1024]{2,1,0:T(8,128)(2,1)S(1)} %collective-permute-done.4.rest_3_.rest_10_), channel_id=1, source_target_pairs={{0,4},{4,0},{8,12},{12,8},{16,20},{20,16},{24,28},{28,24},{1,5},{5... | collective-permute-start | bytes 1769480 | tf_op jit(solution)/shard_map/ppermute | solution.py:60
  62.4 8.4 %copy-start.13 = (bf16[3,96,1024]{2,1,0:T(8,128)(2,1)}, bf16[3,96,1024]{2,1,0:T(8,128)(2,1)S(1)}, u32[]{:S(2)}) copy-start(bf16[3,96,1024]{2,1,0:T(8,128)(2,1)S(1)} %collective-permute-done.3.rest_2_.rest_9_) | copy-start | bytes 1769476
  62.4 7.7 %collective-permute-start.7 = (bf16[3,96,1024]{2,1,0:T(8,128)(2,1)S(1)}, bf16[3,96,1024]{2,1,0:T(8,128)(2,1)S(1)}, u32[]{:S(2)}, u32[]{:S(2)}) collective-permute-start(bf16[3,96,1024]{2,1,0:T(8,128)(2,1)S(1)} %collective-permute-done.3.rest_2_.rest_9_), channel_id=1, source_target_pairs={{0,4},{4,0},{8,12},{12,8},{16,20},{20,16},{24,28},{28,24},{1,5},{5... | collective-permute-start | bytes 1769480 | tf_op jit(solution)/shard_map/ppermute | solution.py:60
  63.0 32.9 %copy-start.5 = (bf16[3,96,1024]{2,1,0:T(8,128)(2,1)}, bf16[3,96,1024]{2,1,0:T(8,128)(2,1)S(1)}, u32[]{:S(2)}) copy-start(bf16[3,96,1024]{2,1,0:T(8,128)(2,1)S(1)} %pad_maximum_fusion.3.rest_1_) | copy-start | bytes 1769476
  63.1 33.3 %collective-permute-start.22 = (bf16[256,1024]{1,0:T(8,128)(2,1)S(1)}, bf16[256,1024]{1,0:T(8,128)(2,1)S(1)}, u32[]{:S(2)}, u32[]{:S(2)}) collective-permute-start(bf16[256,1024]{1,0:T(8,128)(2,1)S(1)} %pad_maximum_fusion.4), channel_id=1, source_target_pairs={{0,3},{1,0},{2,1},{3,2},{4,7},{5,4},{6,5},{7,6},{8,11},{9,8},{10,9... | collective-permute-start | bytes 1572872 | tf_op jit(solution)/shard_map/ppermute | solution.py:55
  67.1 44.8 %collective-permute-start.21 = (bf16[256,1024]{1,0:T(8,128)(2,1)S(1)}, bf16[256,1024]{1,0:T(8,128)(2,1)S(1)}, u32[]{:S(2)}, u32[]{:S(2)}) collective-permute-start(bf16[256,1024]{1,0:T(8,128)(2,1)S(1)} %pad_maximum_fusion.4), channel_id=1, source_target_pairs={{0,2},{1,3},{2,0},{3,1},{4,6},{5,7},{6,4},{7,5},{8,10},{9,11},{10,... | collective-permute-start | bytes 1572872 | tf_op jit(solution)/shard_map/ppermute | solution.py:55
  67.1 3.7 copy-start.14
  67.1 21.3 %collective-permute-start.15 = (bf16[3,96,1024]{2,1,0:T(8,128)(2,1)S(1)}, bf16[3,96,1024]{2,1,0:T(8,128)(2,1)}, u32[]{:S(2)}, u32[]{:S(2)}) collective-permute-start(bf16[3,96,1024]{2,1,0:T(8,128)(2,1)S(1)} %pad_maximum_fusion.3.rest_1_), channel_id=1, source_target_pairs={{0,24},{4,28},{8,16},{12,20},{16,8},{20,12},{24,0},{28,4},{1,25},{... | collective-permute-start | bytes 1769480 | tf_op jit(solution)/shard_map/ppermute | solution.py:60
  68.9 26.9 %collective-permute-start.14 = (bf16[3,96,1024]{2,1,0:T(8,128)(2,1)S(1)}, bf16[3,96,1024]{2,1,0:T(8,128)(2,1)}, u32[]{:S(2)}, u32[]{:S(2)}) collective-permute-start(bf16[3,96,1024]{2,1,0:T(8,128)(2,1)S(1)} %pad_maximum_fusion.3.rest_1_), channel_id=1, source_target_pairs={{0,16},{4,20},{8,24},{12,28},{16,0},{20,4},{24,8},{28,12},{1,17},{... | collective-permute-start | bytes 1769480 | tf_op jit(solution)/shard_map/ppermute | solution.py:60
  70.2 25.8 %collective-permute-start.13 = (bf16[3,96,1024]{2,1,0:T(8,128)(2,1)S(1)}, bf16[3,96,1024]{2,1,0:T(8,128)(2,1)}, u32[]{:S(2)}, u32[]{:S(2)}) collective-permute-start(bf16[3,96,1024]{2,1,0:T(8,128)(2,1)S(1)} %pad_maximum_fusion.3.rest_1_), channel_id=1, source_target_pairs={{0,8},{4,12},{8,0},{12,4},{16,24},{20,28},{24,16},{28,20},{1,9},{5... | collective-permute-start | bytes 1769480 | tf_op jit(solution)/shard_map/ppermute | solution.py:60
  88.4 24.8 %collective-permute-start.20 = (bf16[256,1024]{1,0:T(8,128)(2,1)S(1)}, bf16[256,1024]{1,0:T(8,128)(2,1)S(1)}, u32[]{:S(2)}, u32[]{:S(2)}) collective-permute-start(bf16[256,1024]{1,0:T(8,128)(2,1)S(1)} %pad_maximum_fusion.4), channel_id=1, source_target_pairs={{0,1},{1,2},{2,3},{3,0},{4,5},{5,6},{6,7},{7,4},{8,9},{9,10},{10,1... | collective-permute-start | bytes 1572872 | tf_op jit(solution)/shard_map/ppermute | solution.py:55
  95.9 17.5 %collective-permute-start.16 = (bf16[3,96,1024]{2,1,0:T(8,128)(2,1)S(1)}, bf16[3,96,1024]{2,1,0:T(8,128)(2,1)S(1)}, u32[]{:S(2)}, u32[]{:S(2)}) collective-permute-start(bf16[3,96,1024]{2,1,0:T(8,128)(2,1)S(1)} %pad_maximum_fusion.3.rest_1_), channel_id=1, source_target_pairs={{0,4},{4,0},{8,12},{12,8},{16,20},{20,16},{24,28},{28,24},{1,5},{5... | collective-permute-start | bytes 1769480 | tf_op jit(solution)/shard_map/ppermute | solution.py:60
  96.0 18.4 %collective-permute-start.17 = (bf16[3,96,1024]{2,1,0:T(8,128)(2,1)}, bf16[3,96,1024]{2,1,0:T(8,128)(2,1)S(1)}, u32[]{:S(2)}, u32[]{:S(2)}) collective-permute-start(bf16[3,96,1024]{2,1,0:T(8,128)(2,1)} %collective-permute-done.13.rest_2_), channel_id=1, source_target_pairs={{0,4},{4,0},{8,12},{12,8},{16,20},{20,16},{24,28},{28,24},{1,5},{5... | collective-permute-start | bytes 1769480 | tf_op jit(solution)/shard_map/ppermute | solution.py:60
  96.5 18.7 %collective-permute-start.18 = (bf16[3,96,1024]{2,1,0:T(8,128)(2,1)}, bf16[3,96,1024]{2,1,0:T(8,128)(2,1)S(1)}, u32[]{:S(2)}, u32[]{:S(2)}) collective-permute-start(bf16[3,96,1024]{2,1,0:T(8,128)(2,1)} %collective-permute-done.14.rest_3_), channel_id=1, source_target_pairs={{0,4},{4,0},{8,12},{12,8},{16,20},{20,16},{24,28},{28,24},{1,5},{5... | collective-permute-start | bytes 1769480 | tf_op jit(solution)/shard_map/ppermute | solution.py:60
  111.9 4.1 collective-permute-start.19
  113.4 96.7 %copy-start.2 = (bf16[3,256,1024]{2,1,0:T(8,128)(2,1)}, bf16[3,256,1024]{2,1,0:T(8,128)(2,1)S(1)}, u32[]{:S(2)}) copy-start(bf16[3,256,1024]{2,1,0:T(8,128)(2,1)S(1)} %pad_maximum_fusion.rest_0_) | copy-start | bytes 4718596
  132.7 77.4 %collective-permute-start.25 = (bf16[3,256,1024]{2,1,0:T(8,128)(2,1)S(1)}, bf16[3,256,1024]{2,1,0:T(8,128)(2,1)}, u32[]{:S(2)}, u32[]{:S(2)}) collective-permute-start(bf16[3,256,1024]{2,1,0:T(8,128)(2,1)S(1)} %pad_maximum_fusion.rest_0_), channel_id=1, source_target_pairs={{0,24},{4,28},{8,16},{12,20},{16,8},{20,12},{24,0},{28,4},{1,25},{... | collective-permute-start | bytes 4718600 | tf_op jit(solution)/shard_map/ppermute | solution.py:60
  133.4 76.7 %collective-permute-start.24 = (bf16[3,256,1024]{2,1,0:T(8,128)(2,1)S(1)}, bf16[3,256,1024]{2,1,0:T(8,128)(2,1)}, u32[]{:S(2)}, u32[]{:S(2)}) collective-permute-start(bf16[3,256,1024]{2,1,0:T(8,128)(2,1)S(1)} %pad_maximum_fusion.rest_0_), channel_id=1, source_target_pairs={{0,16},{4,20},{8,24},{12,28},{16,0},{20,4},{24,8},{28,12},{1,17},{... | collective-permute-start | bytes 4718600 | tf_op jit(solution)/shard_map/ppermute | solution.py:60
  138.3 71.8 %collective-permute-start.23 = (bf16[3,256,1024]{2,1,0:T(8,128)(2,1)S(1)}, bf16[3,256,1024]{2,1,0:T(8,128)(2,1)}, u32[]{:S(2)}, u32[]{:S(2)}) collective-permute-start(bf16[3,256,1024]{2,1,0:T(8,128)(2,1)S(1)} %pad_maximum_fusion.rest_0_), channel_id=1, source_target_pairs={{0,8},{4,12},{8,0},{12,4},{16,24},{20,28},{24,16},{28,20},{1,9},{5... | collective-permute-start | bytes 4718600 | tf_op jit(solution)/shard_map/ppermute | solution.py:60
  210.0 35.6 %copy-start.7 = (f32[1,1024]{1,0:T(1,128)S(1)}, f32[1,1024]{1,0:T(1,128)}, u32[]{:S(2)}) copy-start(f32[1,1024]{1,0:T(1,128)} %get-tuple-element.94) | copy-start | bytes 12292
  210.1 35.6 %copy-start.6 = (f32[1,1024]{1,0:T(1,128)S(1)}, f32[1,1024]{1,0:T(1,128)}, u32[]{:S(2)}) copy-start(f32[1,1024]{1,0:T(1,128)} %get-tuple-element.96) | copy-start | bytes 12292
  210.1 37.4 %collective-permute-start.26 = (bf16[3,256,1024]{2,1,0:T(8,128)(2,1)S(1)}, bf16[3,256,1024]{2,1,0:T(8,128)(2,1)}, u32[]{:S(2)}, u32[]{:S(2)}) collective-permute-start(bf16[3,256,1024]{2,1,0:T(8,128)(2,1)S(1)} %pad_maximum_fusion.rest_0_), channel_id=1, source_target_pairs={{0,4},{4,0},{8,12},{12,8},{16,20},{20,16},{24,28},{28,24},{1,5},{5... | collective-permute-start | bytes 4718600 | tf_op jit(solution)/shard_map/ppermute | solution.py:60
  242.9 5.6 collective-permute-start.27
  243.0 7.8 %collective-permute-start.28 = (bf16[3,256,1024]{2,1,0:T(8,128)(2,1)}, bf16[3,256,1024]{2,1,0:T(8,128)(2,1)}, u32[]{:S(2)}, u32[]{:S(2)}) collective-permute-start(bf16[3,256,1024]{2,1,0:T(8,128)(2,1)} %collective-permute-done.24.rest_2_), channel_id=1, source_target_pairs={{0,4},{4,0},{8,12},{12,8},{16,20},{20,16},{24,28},{28,24},{1,5},{5... | collective-permute-start | bytes 4718600 | tf_op jit(solution)/shard_map/ppermute | solution.py:60
  243.4 10.4 %collective-permute-start.29 = (bf16[3,256,1024]{2,1,0:T(8,128)(2,1)}, bf16[3,256,1024]{2,1,0:T(8,128)(2,1)}, u32[]{:S(2)}, u32[]{:S(2)}) collective-permute-start(bf16[3,256,1024]{2,1,0:T(8,128)(2,1)} %collective-permute-done.25.rest_3_), channel_id=1, source_target_pairs={{0,4},{4,0},{8,12},{12,8},{16,20},{20,16},{24,28},{28,24},{1,5},{5... | collective-permute-start | bytes 4718600 | tf_op jit(solution)/shard_map/ppermute | solution.py:60
  245.7 287.4 %all-reduce.8.cloned.1.call-start = ((), (), s32[]{:S(2)}) async-start(), calls=%async_computation | async-start | bytes 4194304 | tf_op jit(solution)/shard_map/psum | solution.py:901
  379.2 56.0 %copy-start.22 = (bf16[2048,1024]{1,0:T(8,128)(2,1)S(1)}, bf16[2048,1024]{1,0:T(8,128)(2,1)}, u32[]{:S(2)}) copy-start(bf16[2048,1024]{1,0:T(8,128)(2,1)} %get-tuple-element.60.x) | copy-start | bytes 12582916
  384.6 63.2 %collective-permute-start.39 = (bf16[66,1024]{1,0:T(8,128)(2,1)S(1)}, bf16[66,1024]{1,0:T(8,128)(2,1)S(1)}, u32[]{:S(2)}, u32[]{:S(2)}) collective-permute-start(bf16[66,1024]{1,0:T(8,128)(2,1)S(1)} %fusion.34), channel_id=1, source_target_pairs={{0,28},{4,24},{8,20},{12,16},{16,12},{20,8},{24,4},{28,0},{1,29},{... | collective-permute-start | bytes 405512 | tf_op jit(solution)/shard_map/ppermute | solution.py:60
  384.8 63.4 %collective-permute-start.33 = (bf16[66,1024]{1,0:T(8,128)(2,1)S(1)}, bf16[66,1024]{1,0:T(8,128)(2,1)S(1)}, u32[]{:S(2)}, u32[]{:S(2)}) collective-permute-start(bf16[66,1024]{1,0:T(8,128)(2,1)S(1)} %get-tuple-element.109), channel_id=1, source_target_pairs={{0,4},{4,0},{8,12},{12,8},{16,20},{20,16},{24,28},{28,24},{1,5},{5... | collective-permute-start | bytes 405512 | tf_op jit(solution)/shard_map/ppermute | solution.py:60
  440.3 9.2 %copy-start.21 = (bf16[2048,1024]{1,0:T(8,128)(2,1)S(1)}, bf16[2048,1024]{1,0:T(8,128)(2,1)}, u32[]{:S(2)}) copy-start(bf16[2048,1024]{1,0:T(8,128)(2,1)} %get-tuple-element.87.gs) | copy-start | bytes 12582916
  443.0 9.7 %collective-permute-start.34 = (bf16[66,1024]{1,0:T(8,128)(2,1)S(1)}, bf16[66,1024]{1,0:T(8,128)(2,1)S(1)}, u32[]{:S(2)}, u32[]{:S(2)}) collective-permute-start(bf16[66,1024]{1,0:T(8,128)(2,1)S(1)} %get-tuple-element.110), channel_id=1, source_target_pairs={{0,8},{4,12},{8,0},{12,4},{16,24},{20,28},{24,16},{28,20},{1,9},{5... | collective-permute-start | bytes 405512 | tf_op jit(solution)/shard_map/ppermute | solution.py:60
  444.9 7.9 %collective-permute-start.35 = (bf16[66,1024]{1,0:T(8,128)(2,1)S(1)}, bf16[66,1024]{1,0:T(8,128)(2,1)S(1)}, u32[]{:S(2)}, u32[]{:S(2)}) collective-permute-start(bf16[66,1024]{1,0:T(8,128)(2,1)S(1)} %get-tuple-element.111), channel_id=1, source_target_pairs={{0,12},{4,8},{8,4},{12,0},{16,28},{20,24},{24,20},{28,16},{1,13},{... | collective-permute-start | bytes 405512 | tf_op jit(solution)/shard_map/ppermute | solution.py:60
  445.1 10.0 %collective-permute-start.36 = (bf16[66,1024]{1,0:T(8,128)(2,1)S(1)}, bf16[66,1024]{1,0:T(8,128)(2,1)S(1)}, u32[]{:S(2)}, u32[]{:S(2)}) collective-permute-start(bf16[66,1024]{1,0:T(8,128)(2,1)S(1)} %get-tuple-element.112), channel_id=1, source_target_pairs={{0,16},{4,20},{8,24},{12,28},{16,0},{20,4},{24,8},{28,12},{1,17},{... | collective-permute-start | bytes 405512 | tf_op jit(solution)/shard_map/ppermute | solution.py:60
  447.8 11.0 %collective-permute-start.37 = (bf16[66,1024]{1,0:T(8,128)(2,1)S(1)}, bf16[66,1024]{1,0:T(8,128)(2,1)S(1)}, u32[]{:S(2)}, u32[]{:S(2)}) collective-permute-start(bf16[66,1024]{1,0:T(8,128)(2,1)S(1)} %get-tuple-element.113), channel_id=1, source_target_pairs={{0,20},{4,16},{8,28},{12,24},{16,4},{20,0},{24,12},{28,8},{1,21},{... | collective-permute-start | bytes 405512 | tf_op jit(solution)/shard_map/ppermute | solution.py:60
  448.2 4.5 copy-start.9
  448.2 10.6 %collective-permute-start.38 = (bf16[66,1024]{1,0:T(8,128)(2,1)S(1)}, bf16[66,1024]{1,0:T(8,128)(2,1)S(1)}, u32[]{:S(2)}, u32[]{:S(2)}) collective-permute-start(bf16[66,1024]{1,0:T(8,128)(2,1)S(1)} %get-tuple-element.114), channel_id=1, source_target_pairs={{0,24},{4,28},{8,16},{12,20},{16,8},{20,12},{24,0},{28,4},{1,25},{... | collective-permute-start | bytes 405512 | tf_op jit(solution)/shard_map/ppermute | solution.py:60
  452.8 84.6 %collective-permute-start.32 = (bf16[512,1024]{1,0:T(8,128)(2,1)S(1)}, bf16[512,1024]{1,0:T(8,128)(2,1)}, u32[]{:S(2)}, u32[]{:S(2)}) collective-permute-start(bf16[512,1024]{1,0:T(8,128)(2,1)S(1)} %copy-done.9), channel_id=1, source_target_pairs={{0,3},{1,0},{2,1},{3,2},{4,7},{5,4},{6,5},{7,6},{8,11},{9,8},{10,9... | collective-permute-start | bytes 3145736 | tf_op jit(solution)/shard_map/ppermute | solution.py:55
  452.8 92.0 %collective-permute-start.31 = (bf16[512,1024]{1,0:T(8,128)(2,1)S(1)}, bf16[512,1024]{1,0:T(8,128)(2,1)}, u32[]{:S(2)}, u32[]{:S(2)}) collective-permute-start(bf16[512,1024]{1,0:T(8,128)(2,1)S(1)} %copy-done.9), channel_id=1, source_target_pairs={{0,2},{1,3},{2,0},{3,1},{4,6},{5,7},{6,4},{7,5},{8,10},{9,11},{10,... | collective-permute-start | bytes 3145736 | tf_op jit(solution)/shard_map/ppermute | solution.py:55
  455.1 89.7 %collective-permute-start.30 = (bf16[512,1024]{1,0:T(8,128)(2,1)S(1)}, bf16[512,1024]{1,0:T(8,128)(2,1)}, u32[]{:S(2)}, u32[]{:S(2)}) collective-permute-start(bf16[512,1024]{1,0:T(8,128)(2,1)S(1)} %copy-done.9), channel_id=1, source_target_pairs={{0,1},{1,2},{2,3},{3,0},{4,5},{5,6},{6,7},{7,4},{8,9},{9,10},{10,1... | collective-permute-start | bytes 3145736 | tf_op jit(solution)/shard_map/ppermute | solution.py:55
  459.1 9.7 %collective-permute-start.40 = (bf16[66,1024]{1,0:T(8,128)(2,1)S(1)}, bf16[66,1024]{1,0:T(8,128)(2,1)S(1)}, u32[]{:S(2)}, u32[]{:S(2)}) collective-permute-start(bf16[66,1024]{1,0:T(8,128)(2,1)S(1)} %get-tuple-element.108), channel_id=1, source_target_pairs={{0,4},{4,0},{8,12},{12,8},{16,20},{20,16},{24,28},{28,24},{1,5},{5... | collective-permute-start | bytes 405512 | tf_op jit(solution)/shard_map/ppermute | solution.py:60
  460.6 4.2 copy-start.1
  467.3 35.0 %collective-permute-start.45 = (bf16[66,1024]{1,0:T(8,128)(2,1)S(1)}, bf16[66,1024]{1,0:T(8,128)(2,1)S(1)}, u32[]{:S(2)}, u32[]{:S(2)}) collective-permute-start(bf16[66,1024]{1,0:T(8,128)(2,1)S(1)} %get-tuple-element.108), channel_id=1, source_target_pairs={{0,24},{4,28},{8,16},{12,20},{16,8},{20,12},{24,0},{28,4},{1,25},{... | collective-permute-start | bytes 405512 | tf_op jit(solution)/shard_map/ppermute | solution.py:60
  468.8 14.7 %collective-permute-start.41 = (bf16[66,1024]{1,0:T(8,128)(2,1)S(1)}, bf16[66,1024]{1,0:T(8,128)(2,1)S(1)}, u32[]{:S(2)}, u32[]{:S(2)}) collective-permute-start(bf16[66,1024]{1,0:T(8,128)(2,1)S(1)} %get-tuple-element.108), channel_id=1, source_target_pairs={{0,8},{4,12},{8,0},{12,4},{16,24},{20,28},{24,16},{28,20},{1,9},{5... | collective-permute-start | bytes 405512 | tf_op jit(solution)/shard_map/ppermute | solution.py:60
  483.5 5.9 %collective-permute-start.42 = (bf16[66,1024]{1,0:T(8,128)(2,1)S(1)}, bf16[66,1024]{1,0:T(8,128)(2,1)S(1)}, u32[]{:S(2)}, u32[]{:S(2)}) collective-permute-start(bf16[66,1024]{1,0:T(8,128)(2,1)S(1)} %get-tuple-element.108), channel_id=1, source_target_pairs={{0,12},{4,8},{8,4},{12,0},{16,28},{20,24},{24,20},{28,16},{1,13},{... | collective-permute-start | bytes 405512 | tf_op jit(solution)/shard_map/ppermute | solution.py:60
  489.3 5.4 collective-permute-start.43
  494.7 6.1 %collective-permute-start.44 = (bf16[66,1024]{1,0:T(8,128)(2,1)S(1)}, bf16[66,1024]{1,0:T(8,128)(2,1)S(1)}, u32[]{:S(2)}, u32[]{:S(2)}) collective-permute-start(bf16[66,1024]{1,0:T(8,128)(2,1)S(1)} %get-tuple-element.108), channel_id=1, source_target_pairs={{0,20},{4,16},{8,28},{12,24},{16,4},{20,0},{24,12},{28,8},{1,21},{... | collective-permute-start | bytes 405512 | tf_op jit(solution)/shard_map/ppermute | solution.py:60
  500.8 6.8 %collective-permute-start.46 = (bf16[66,1024]{1,0:T(8,128)(2,1)S(1)}, bf16[66,1024]{1,0:T(8,128)(2,1)S(1)}, u32[]{:S(2)}, u32[]{:S(2)}) collective-permute-start(bf16[66,1024]{1,0:T(8,128)(2,1)S(1)} %get-tuple-element.108), channel_id=1, source_target_pairs={{0,28},{4,24},{8,20},{12,16},{16,12},{20,8},{24,4},{28,0},{1,29},{... | collective-permute-start | bytes 405512 | tf_op jit(solution)/shard_map/ppermute | solution.py:60
  (8 other events, 11.3 us)
Sparse Core Ops, SparseCore 0:
  245.9 80.2 all-reduce.9
  467.4 65.6 all-reduce.7
